TPU v7x, 256 devices: a whole 4x4x8 slice. The times are simulated.
256 devices in a mesh: acq: 16 (over y, x), rows: 16 (over z, core).
Axes of the slice: x: 4, y: 4, z: 8, core: 2. Of those that a mesh axis runs over, the one named last changes fastest.
Arguments:
- slc: float32 [16, 2, 512, 4096], P('acq', None, 'rows'), may hold values from -6 to 6
- pair_index: int32 [16, 2], P('acq'), may hold values from 0 to 15, as said below
Outputs:
- products: float32 [16, 3, 512, 4096], P('acq', None, 'rows')
Inputs may be any that keep to these rules, and one draw needn't show every extreme that they name: `pair_index`: pair p has reference acquisition p mod 16 and a secondary acquisition different from it.
All inputs are finite; a program needn't handle non-finite values.
Results may differ from a plain program's by a relative error of at most 0.00009.
Values sent between devices are 32-bit elements; how exact they have to be, the bound alone decides.
No kernel may reach another device: no remote copies, remote signals or barrier semaphores. Data moves between devices by JAX's collectives and lax.ppermute only.
A program may use at most 64 MiB of HBM per device.

v0:
```python
import math

import jax
import jax.numpy as jnp
from jax import lax
from jax.sharding import PartitionSpec as P

LOOK_R = 5
LOOK_C = 19
PATCH = 32


def extended_2(cells, sides, width):
    for axis, dim in sides:
        count = lax.axis_size(axis)
        ends = count - 1
        head = lax.slice_in_dim(cells, 0, width, axis=dim)
        tail = lax.slice_in_dim(cells, cells.shape[dim] - width, cells.shape[dim], axis=dim)
        cells = jnp.concatenate(
            [
                lax.ppermute(tail, axis, [(i, (i + 1) % count) for i in range(ends)]),
                cells,
                lax.ppermute(head, axis, [((i + 1) % count, i) for i in range(ends)]),
            ],
            axis=dim,
        )
    return cells


def boxsum(field, rows_out, cols_out):
    total = field[..., 0:rows_out, :]
    for shift in range(1, LOOK_R):
        total = total + field[..., shift : shift + rows_out, :]
    result = total[..., :, 0:cols_out]
    for shift in range(1, LOOK_C):
        result = result + total[..., :, shift : shift + cols_out]
    return result


def left_mul(matrix, field):
    return jnp.einsum("ij,ajbk->aibk", matrix, field, precision=lax.Precision.HIGHEST)


def right_mul(field, matrix):
    return jnp.einsum("ajbk,kl->ajbl", field, matrix, precision=lax.Precision.HIGHEST)


def goldstein(real_part, imag_part):
    height, width = real_part.shape
    index = jnp.arange(PATCH, dtype=jnp.int32)
    phase = 2.0 * math.pi / PATCH * (index[:, None] * index[None, :] % PATCH).astype(jnp.float32)
    cosine = jnp.cos(phase)
    sine = jnp.sin(phase)
    xr = real_part.reshape(height // PATCH, PATCH, width // PATCH, PATCH)
    xi = imag_part.reshape(height // PATCH, PATCH, width // PATCH, PATCH)
    yr = left_mul(cosine, xr) + left_mul(sine, xi)
    yi = left_mul(cosine, xi) - left_mul(sine, xr)
    zr = right_mul(yr, cosine) + right_mul(yi, sine)
    zi = right_mul(yi, cosine) - right_mul(yr, sine)
    weight = jnp.sqrt(jnp.sqrt(zr * zr + zi * zi + 1e-06))
    weight = weight / jnp.mean(weight, axis=(1, 3), keepdims=True)
    ur = zr * weight
    ui = zi * weight
    vr = left_mul(cosine, ur) - left_mul(sine, ui)
    vi = left_mul(cosine, ui) + left_mul(sine, ur)
    scale = 1.0 / (PATCH * PATCH)
    out_re = (right_mul(vr, cosine) - right_mul(vi, sine)) * scale
    out_im = (right_mul(vi, cosine) + right_mul(vr, sine)) * scale
    return (out_re.reshape(height, width), out_im.reshape(height, width))


def pair_terms(first, second):
    rows_out = first.shape[1] - (LOOK_R - 1)
    cols_out = first.shape[2] - (LOOK_C - 1)
    cross_re = first[0] * second[0] + first[1] * second[1]
    cross_im = first[1] * second[0] - first[0] * second[1]
    power_a = first[0] * first[0] + first[1] * first[1]
    power_b = second[0] * second[0] + second[1] * second[1]
    sums = boxsum(jnp.stack([cross_re, cross_im, power_a, power_b]), rows_out, cols_out)
    scale = lax.rsqrt(sums[2] * sums[3] + 1e-06)
    gamma_re = sums[0] * scale
    gamma_im = sums[1] * scale
    coherence = jnp.sqrt(gamma_re * gamma_re + gamma_im * gamma_im)
    filt_re, filt_im = goldstein(gamma_re, gamma_im)
    return jnp.stack([coherence, filt_re, filt_im])


def on_device(slc, pair_index):
    half_r = (LOOK_R - 1) // 2
    half_c = (LOOK_C - 1) // 2
    extended = extended_2(slc, (("rows", 2),), half_r)
    stacked = lax.all_gather(extended, "acq", axis=0, tiled=True)

    def single(pair):
        first = jnp.pad(stacked[pair[0]], ((0, 0), (0, 0), (half_c, half_c)))
        second = jnp.pad(stacked[pair[1]], ((0, 0), (0, 0), (half_c, half_c)))
        return pair_terms(first, second)

    return jax.vmap(single)(pair_index)


def solution(mesh):
    return jax.shard_map(
        on_device,
        mesh=mesh,
        in_specs=(P("acq", None, "rows", None), P("acq", None)),
        out_specs=P("acq", None, "rows", None),
        check_vma=False,
    )
```

profile of v0, /device:TPU:97, one launch (start us, length us, event | category | flops | bytes accessed | tf_op | source)
XLA Modules:
  0.0 199.6 jit_solution(16915045263950061631)
XLA Ops:
  6.5 0.0 all-gather.2.cloned.1.call-start
  6.5 2.0 %copy.56 = f32[1,2,32,4096]{3,1,2,0:T(2,128)S(1)} copy(f32[1,2,32,4096]{3,2,1,0:T(8,128)} %param.2) | data formatting | bytes 2097152 | tf_op args[0]
  8.6 0.0 copy-start.2
  8.6 5.3 %collective-permute-start = (f32[1,2,2,4096]{3,1,2,0:T(2,128)S(1)}, f32[1,2,2,4096]{3,1,2,0:T(2,128)S(1)}, u32[]{:S(2)}, u32[]{:S(2)}) collective-permute-start(f32[1,2,2,4096]{3,1,2,0:T(2,128)S(1)} %get-tuple-element.38), channel_id=1, source_target_pairs={{0,1},{1,2},{2,3},{3,4},{4,5},{5,6},{6,7},{7,8},{8,9},{9,10},{10,1... | collective-permute-start | bytes 196616 | tf_op jit(solution)/shard_map/ppermute | solution.py:21
  13.9 1.9 collective-permute-start.1
  15.9 0.0 collective-permute-done
  15.9 4.9 %collective-permute-done.1 = f32[1,2,2,4096]{3,1,2,0:T(2,128)S(1)} collective-permute-done((f32[1,2,2,4096]{3,1,2,0:T(2,128)S(1)}, f32[1,2,2,4096]{3,1,2,0:T(2,128)S(1)}, u32[]{:S(2)}, u32[]{:S(2)}) %collective-permute-start.1) | collective-permute-done | bytes 65568 | tf_op jit(solution)/shard_map/ppermute | solution.py:23
  20.7 1.6 pad_maximum_fusion.1
  22.3 0.0 all-gather.2.cloned.1.call-update
  22.4 0.0 copy-done.2
  22.4 0.6 fusion.136
  26.7 121.6 %all-gather.2.cloned.1.call-done = f32[16,2,36,4096]{3,1,2,0:T(2,128)} async-done(((f32[1,2,36,4096]{3,1,2,0:T(2,128)}), f32[16,2,36,4096]{3,1,2,0:T(2,128)}) %all-gather.2.cloned.1.call-update) | async-done | bytes 18874384 | tf_op jit(solution)/shard_map/all_gather | solution.py:92
  148.4 1.8 constant_dynamic-slice_fusion
  150.1 0.7 copy.103
  150.8 0.7 copy.104
  151.5 2.2 %multiply_add_fusion.2 = (f32[1,1,36,4114]{3,2,1,0:T(8,128)S(1)}, f32[1,1,36,4114]{3,2,1,0:T(8,128)S(1)}, f32[1,1,36,4114]{3,2,1,0:T(8,128)S(1)}, f32[1,1,36,4114]{3,2,1,0:T(8,128)S(1)}) fusion(f32[1,2,36,4096]{3,2,1,0:T(8,128)S(1)} %copy.103, f32[1,2,36,4096]{3,2,1,0:T(8,128)S(1)} %copy.104), kind=kLoop, calls=%fused_computation.46 | loop fusion | flops 1777248 | bytes 4728960 | tf_op jit(solution)/shard_map/vmap()/add | solution.py:75
  153.7 0.3 pad_maximum_fusion
  153.9 0.8 slice_add_fusion
  154.8 10.1 %slice_add_fusion.4 = f32[4,1,32,4096]{3,2,1,0:T(8,128)S(1)} fusion(f32[4,1,32,4114]{3,2,1,0:T(8,128)S(1)} %slice_add_fusion), kind=kLoop, calls=%fused_computation.5 | loop fusion | flops 9437184 | bytes 41943040 | tf_op jit(solution)/shard_map/vmap()/add | solution.py:36
  164.8 1.1 add_sqrt_fusion
  165.9 0.7 mul.277
  166.6 0.7 copy.61
  167.3 1.5 fusion.48
  168.8 0.7 mul.283
  169.5 0.7 copy.63
  170.2 0.7 fusion.42
  170.9 1.7 fusion.5
  172.7 0.7 fusion.4
  173.4 0.9 fusion.20
  174.3 0.9 fusion.24
  175.3 1.0 convolution_add_fusion.2
  176.2 1.2 fusion.28
  177.5 0.4 fusion.27
  177.9 1.0 fusion.18
  178.8 1.0 fusion.14
  179.8 1.2 fusion.3
  181.0 1.0 fusion.2
  182.0 0.9 fusion.8
  182.9 0.9 fusion.12
  183.8 0.9 fusion
  184.8 0.9 fusion.1
  185.8 0.6 copy.83
  186.4 1.8 reshape.169
  188.1 0.0 copy-start
  188.1 0.6 copy.86
  188.7 0.0 copy-start.1
  188.7 1.8 reshape.170
  190.5 0.0 copy-done
  190.5 0.0 copy-done.1
  190.5 2.3 %maximum_bitcast_fusion = f32[1,3,32,4096]{3,2,1,0:T(8,128)} fusion(f32[1,1,32,4096]{3,2,1,0:T(8,128)} %reshape.170, f32[1,1,32,4096]{3,2,1,0:T(8,128)S(1)} %copy-done.1, f32[1,1,32,4096]{3,2,1,0:T(8,128)S(1)} %copy-done), kind=kLoop, calls=%fused_computation.23 | loop fusion | flops 786432 | bytes 3145728 | tf_op jit(solution)/shard_map/vmap()/transpose | solution.py:99
  (2 shorter events, 0.0 us)
Async XLA Ops:
  6.5 141.8 %all-gather.2.cloned.1.call-start = ((), (), s32[]{:S(2)}) async-start(), calls=%async_computation | async-start | bytes 20054016 | tf_op jit(solution)/shard_map/all_gather | solution.py:92
  8.6 13.8 %copy-start.2 = (s32[1,2]{1,0:T(1,128)S(1)}, s32[1,2]{1,0:T(1,128)}, u32[]{:S(2)}) copy-start(s32[1,2]{1,0:T(1,128)} %param.3) | copy-start | bytes 28
  8.6 7.3 %collective-permute-start = (f32[1,2,2,4096]{3,1,2,0:T(2,128)S(1)}, f32[1,2,2,4096]{3,1,2,0:T(2,128)S(1)}, u32[]{:S(2)}, u32[]{:S(2)}) collective-permute-start(f32[1,2,2,4096]{3,1,2,0:T(2,128)S(1)} %get-tuple-element.38), channel_id=1, source_target_pairs={{0,1},{1,2},{2,3},{3,4},{4,5},{5,6},{6,7},{7,8},{8,9},{9,10},{10,1... | collective-permute-start | bytes 196616 | tf_op jit(solution)/shard_map/ppermute | solution.py:21
  13.9 6.8 %collective-permute-start.1 = (f32[1,2,2,4096]{3,1,2,0:T(2,128)S(1)}, f32[1,2,2,4096]{3,1,2,0:T(2,128)S(1)}, u32[]{:S(2)}, u32[]{:S(2)}) collective-permute-start(f32[1,2,2,4096]{3,1,2,0:T(2,128)S(1)} %get-tuple-element.39), channel_id=1, source_target_pairs={{1,0},{2,1},{3,2},{4,3},{5,4},{6,5},{7,6},{8,7},{9,8},{10,9},{11,1... | collective-permute-start | bytes 196616 | tf_op jit(solution)/shard_map/ppermute | solution.py:23
  188.1 2.4 %copy-start = (f32[1,1,32,4096]{3,2,1,0:T(8,128)S(1)}, f32[1,1,32,4096]{3,2,1,0:T(8,128)}, u32[]{:S(2)}) copy-start(f32[1,1,32,4096]{3,2,1,0:T(8,128)} %get-tuple-element.27) | copy-start | bytes 1572868
  188.7 1.8 copy-start.1
Sparse Core Ops, SparseCore 0:
  22.5 125.8 all-gather.1
where the time goes:
time: 202 us; the launch traced here: 200 us
  waiting for transfers between devices  127 us (63%)
  other arithmetic  18.6 us (9%)
  between operations  17.4 us (9%)
  matrix products  16.5 us (8%)
  local copies, waits for them, and re-layouts  13.3 us (7%)
  starting transfers between devices  7.24 us (4%)
    all_gather x1, waiting for transfers between devices, on_device(): stacked = lax.all_gather(extended, 'acq', axis=0, tiled=True)  122 us
    add x1, other arithmetic, boxsum(): result = result + total[..., :, shift:shift + cols_out]  10.1 us
    dot_general x8, matrix products, left_mul(): jnp.einsum('ij,ajbk->aibk', matrix, field, precision=lax.Precision.HIGHEST)  8.71 us
    dot_general x8, matrix products, right_mul(): jnp.einsum('ajbk,kl->ajbl', field, matrix, precision=lax.Precision.HIGHEST)  7.81 us
    ppermute x1, starting transfers between devices, extended_2(): lax.ppermute(tail, axis, [(i, (i + 1) % count) for i in range(ends)])  5.32 us
    ppermute x1, waiting for transfers between devices, extended_2(): lax.ppermute(head, axis, [((i + 1) % count, i) for i in range(ends)])  4.86 us
  transfers between devices with their start and end apart: 3, of which 2 were waited for; matrix products, arithmetic and copies ran while one was open for 0% of the time, Pallas kernels for 0%

commit v1 on v0

v1 whole, which is shorter than its diff:
```python
import functools

import jax
import jax.numpy as jnp
import ml_dtypes
import numpy as np
from jax import lax
from jax.experimental import pallas as pl
from jax.experimental.pallas import tpu as pltpu
from jax.sharding import PartitionSpec as P

LOOK_R = 5
LOOK_C = 19
PATCH = 32
LANES = 128
BLOCK = 256
VMEM = pl.BlockSpec(memory_space=pltpu.VMEM)
SMEM = pl.BlockSpec(memory_space=pltpu.SMEM)
PARAMS = pltpu.CompilerParams(vmem_limit_bytes=40 * 1024 * 1024)
F32 = jnp.float32
BF16 = jnp.bfloat16


def cost(flops, moved):
    return pl.CostEstimate(flops=flops, bytes_accessed=moved, transcendentals=0)


def halves(matrix):
    high = matrix.astype(ml_dtypes.bfloat16)
    low = (matrix - high.astype(np.float64)).astype(ml_dtypes.bfloat16)
    return high, low


def split(x):
    high = x.astype(BF16)
    low = (x - high.astype(F32)).astype(BF16)
    return high, low


def constants():
    index = np.arange(PATCH)
    phase = 2.0 * np.pi / PATCH * (index[:, None] * index[None, :] % PATCH)
    c, s = np.cos(phase), np.sin(phase)
    eye = np.eye(LANES // PATCH)
    cb, sb = np.kron(eye, c), np.kron(eye, s)

    def three_rows(m):
        h, l = halves(m)
        return np.concatenate([h, h, l], axis=0)

    def three_cols(m):
        h, l = halves(m)
        return np.concatenate([h, h, l], axis=1)

    right = three_rows(np.block([[cb, -sb], [sb, cb]]))
    right_inv = three_rows(np.block([[cb, sb], [-sb, cb]]) / (PATCH * PATCH))
    left = three_cols(np.block([[c, s], [-s, c]]))
    left_inv = three_cols(np.block([[c, -s], [s, c]]))
    half = LOOK_C // 2
    row, col = np.arange(BLOCK)[:, None], np.arange(BLOCK)[None, :]
    near = (np.abs(row - LANES - col) <= half).astype(ml_dtypes.bfloat16)
    far = (np.abs(row + LANES - col) <= half).astype(ml_dtypes.bfloat16)
    band = np.concatenate([near, near, far, far], axis=0)
    mean = np.kron(np.eye(BLOCK // PATCH), np.full((PATCH, PATCH), 1.0 / (PATCH * PATCH))).astype(ml_dtypes.bfloat16)
    mean = np.concatenate([mean, mean], axis=0)
    return right, right_inv, left, left_inv, band, mean


def spread_chunks(slc, pair_index):
    count = slc.shape[3] // BLOCK

    def kernel(x_ref, pair_ref, o_ref):
        wanted = jnp.full((8, LANES), pair_ref[0, 1].astype(F32))
        for j in range(count):
            for k in range(2):
                cols = slice(BLOCK * j + LANES * k, BLOCK * j + LANES * (k + 1))
                for c in range(2):
                    o_ref[j, 64 * k + 32 * c : 64 * k + 32 * c + 32] = x_ref[0, c, :, cols]
            o_ref[j, 128:136] = wanted

    return pl.pallas_call(
        kernel,
        out_shape=jax.ShapeDtypeStruct((count, 136, LANES), F32),
        in_specs=[VMEM, SMEM],
        out_specs=VMEM,
        compiler_params=PARAMS,
        cost_estimate=cost(0, 2 << 20),
        name="spread_chunks",
    )(slc, pair_index)


def pick_chunks(held):
    count = held.shape[0]

    def kernel(v_ref, o_ref):
        for p in range(count):
            wanted = v_ref[p, 128:129, 0:1][0, 0].astype(jnp.int32)
            o_ref[p] = v_ref[wanted, 0:128]

    return pl.pallas_call(
        kernel,
        out_shape=jax.ShapeDtypeStruct((count, 128, LANES), F32),
        in_specs=[VMEM],
        out_specs=VMEM,
        compiler_params=PARAMS,
        cost_estimate=cost(0, 2 << 20),
        name="pick_chunks",
    )(held)


def edge_rows(slc, second, core):
    count = second.shape[0]

    def kernel(core_ref, a_ref, b_ref, near_ref, away_ref):
        even = core_ref[0] == 0
        for j in range(count):
            for k in range(2):
                cols = slice(BLOCK * j + LANES * k, BLOCK * j + LANES * (k + 1))
                for c in range(2):
                    at = slice(4 * c + 2 * k, 4 * c + 2 * k + 2)
                    base = 64 * k + 32 * c
                    for i, (top, low) in enumerate((
                        (a_ref[0, c, 0:2, cols], a_ref[0, c, 30:32, cols]),
                        (b_ref[j, base : base + 2], b_ref[j, base + 30 : base + 32]),
                    )):
                        near_ref[i, j, at] = jnp.where(even, low, top)
                        away_ref[i, j, at] = jnp.where(even, top, low)

    shape = jax.ShapeDtypeStruct((2, count, 8, LANES), F32)
    return pl.pallas_call(
        kernel,
        out_shape=(shape, shape),
        in_specs=[SMEM, VMEM, VMEM],
        out_specs=(VMEM, VMEM),
        compiler_params=PARAMS,
        cost_estimate=cost(0, 2 << 20),
        name="edge_rows",
    )(core, slc, second)


def own_sums(slc, second, band):
    count = second.shape[0]

    def kernel(a_ref, b_ref, w_ref, o_ref, rows_ref, high_ref, low_ref):
        zero8 = jnp.zeros((8, LANES), F32)
        for slot in range(8):
            rows_ref[slot, 0:8] = zero8
            rows_ref[slot, 40:48] = zero8
        zero = jnp.zeros((128, LANES), BF16)
        for ref in (high_ref, low_ref):
            ref[0, :, 0:LANES] = zero
            ref[count, :, LANES:BLOCK] = zero
        for t in range(2 * count):
            j, k = t // 2, t % 2
            cols = slice(LANES * t, LANES * (t + 1))
            a0, a1 = a_ref[0, 0, :, cols], a_ref[0, 1, :, cols]
            b0, b1 = b_ref[j, 64 * k : 64 * k + 32], b_ref[j, 64 * k + 32 : 64 * k + 64]
            fields = (a0 * b0 + a1 * b1, a1 * b0 - a0 * b1, a0 * a0 + a1 * a1, b0 * b0 + b1 * b1)
            at, side = (t + 1) // 2, (t + 1) % 2
            lanes = slice(LANES * side, LANES * (side + 1))
            for f, field in enumerate(fields):
                slot = 4 * (t % 2) + f
                rows_ref[slot, 8:40] = field
                total = field
                for shift in (6, 7, 9, 10):
                    total = total + rows_ref[slot, shift : shift + 32]
                high, low = split(total)
                high_ref[at, 32 * f : 32 * f + 32, lanes] = high
                low_ref[at, 32 * f : 32 * f + 32, lanes] = low
        for j in range(count):
            left = jnp.concatenate([high_ref[j], low_ref[j], high_ref[j + 1], low_ref[j + 1]], axis=1)
            o_ref[j] = jnp.dot(left, w_ref[...], preferred_element_type=F32)

    return pl.pallas_call(
        kernel,
        out_shape=jax.ShapeDtypeStruct((count, 128, BLOCK), F32),
        in_specs=[VMEM, VMEM, VMEM],
        out_specs=VMEM,
        scratch_shapes=[
            pltpu.VMEM((8, 48, LANES), F32),
            pltpu.VMEM((count + 1, 128, BLOCK), BF16),
            pltpu.VMEM((count + 1, 128, BLOCK), BF16),
        ],
        compiler_params=PARAMS,
        cost_estimate=cost(4 << 30, 8 << 20),
        name="own_sums",
    )(slc, second, band)


def filtered(sums, near, away, core, right, right_inv, left, left_inv, band, mean):
    count = sums.shape[0]

    def kernel(core_ref, s_ref, near_ref, away_ref, r_ref, ri_ref, l_ref, li_ref, w_ref, m_ref, o_ref,
               edge_ref, gh_ref, gl_ref, y_ref, vh_ref, vl_ref, sum_ref):
        even = core_ref[0] == 0
        sub = lax.broadcasted_iota(jnp.int32, (8, LANES), 0)
        odd_row = sub % 2 == 1
        edge_ref[...] = jnp.zeros(edge_ref.shape, F32)
        for j in range(count):
            for place in range(2):
                if place == 0:
                    pick = lambda i: jnp.where(even, away_ref[i, j], near_ref[i, j])
                else:
                    pick = lambda i: jnp.where(even, near_ref[i, j], away_ref[i, j])
                a, b = pick(0), pick(1)
                turned = pltpu.roll(b, 4, 0)
                mixed = a * turned
                same, aa, bb = a * b, a * a, b * b
                fields = (
                    same + pltpu.roll(same, 4, 0),
                    pltpu.roll(mixed, 4, 0) - mixed,
                    aa + pltpu.roll(aa, 4, 0),
                    bb + pltpu.roll(bb, 4, 0),
                )
                for f, field in enumerate(fields):
                    if place == 0:
                        field = jnp.where(odd_row, field, field + pltpu.roll(field, 7, 0))
                    else:
                        field = jnp.where(odd_row, field + pltpu.roll(field, 1, 0), field)
                    row = 8 * f + 6 * place
                    edge_ref[j, row : row + 2, LANES:BLOCK] = field[0:2]
                    edge_ref[j + 1, row : row + 2, 0:LANES] = field[2:4]
        top_half = lax.broadcasted_iota(jnp.int32, (8, BLOCK), 0) < 4
        for j in range(count):
            h0, l0 = split(edge_ref[j])
            h1, l1 = split(edge_ref[j + 1])
            more = jnp.dot(jnp.concatenate([h0, l0, h1, l1], axis=1), w_ref[...], preferred_element_type=F32)
            total = []
            for f in range(4):
                extra = more[8 * f : 8 * f + 8]
                first = s_ref[j, 32 * f : 32 * f + 8] + jnp.where(top_half, extra, 0.0)
                last = s_ref[j, 32 * f + 24 : 32 * f + 32] + jnp.where(top_half, 0.0, extra)
                total.append(jnp.concatenate([first, s_ref[j, 32 * f + 8 : 32 * f + 24], last], axis=0))
            scale = lax.rsqrt(total[2] * total[3] + 1e-06)
            gr, gi = total[0] * scale, total[1] * scale
            o_ref[0, 0, :, BLOCK * j : BLOCK * (j + 1)] = jnp.sqrt(gr * gr + gi * gi)
            rh, rl = split(gr)
            ih, il = split(gi)
            for k in range(2):
                at, cols = slice(64 * j + 32 * k, 64 * j + 32 * k + 32), slice(LANES * k, LANES * (k + 1))
                gh_ref[at, 0:LANES] = rh[:, cols]
                gh_ref[at, LANES:BLOCK] = ih[:, cols]
                gl_ref[at, 0:LANES] = rl[:, cols]
                gl_ref[at, LANES:BLOCK] = il[:, cols]
        step = 256
        for m in range(0, 64 * count, step):
            h, l = gh_ref[m : m + step], gl_ref[m : m + step]
            y_ref[m : m + step] = jnp.dot(jnp.concatenate([h, l, h], axis=1), r_ref[...], preferred_element_type=F32)
        for j in range(count):
            one, two = slice(64 * j, 64 * j + 32), slice(64 * j + 32, 64 * j + 64)
            yr = jnp.concatenate([y_ref[one, 0:LANES], y_ref[two, 0:LANES]], axis=1)
            yi = jnp.concatenate([y_ref[one, LANES:BLOCK], y_ref[two, LANES:BLOCK]], axis=1)
            h, l = split(jnp.concatenate([yr, yi], axis=0))
            z = jnp.dot(l_ref[...], jnp.concatenate([h, l, h], axis=0), preferred_element_type=F32)
            zr, zi = z[0:32], z[32:64]
            weight = lax.rsqrt(lax.rsqrt(zr * zr + zi * zi + 1e-06))
            sum_ref[j : j + 1] = jnp.sum(weight, axis=0, keepdims=True)
            h, l = split(jnp.concatenate([zr * weight, zi * weight], axis=0))
            v = jnp.dot(li_ref[...], jnp.concatenate([h, l, h], axis=0), preferred_element_type=F32)
            h, l = split(v)
            for ref, part in ((vh_ref, h), (vl_ref, l)):
                ref[one, 0:LANES] = part[0:32, 0:LANES]
                ref[one, LANES:BLOCK] = part[32:64, 0:LANES]
                ref[two, 0:LANES] = part[0:32, LANES:BLOCK]
                ref[two, LANES:BLOCK] = part[32:64, LANES:BLOCK]
        h, l = split(sum_ref[...])
        inverse = 1.0 / jnp.dot(jnp.concatenate([h, l], axis=1), m_ref[...], preferred_element_type=F32)
        sum_ref[...] = inverse
        for m in range(0, 64 * count, step):
            h, l = vh_ref[m : m + step], vl_ref[m : m + step]
            out = jnp.dot(jnp.concatenate([h, l, h], axis=1), ri_ref[...], preferred_element_type=F32)
            for n in range(step // 32):
                t = m // 32 + n
                factor = sum_ref[t // 2 : t // 2 + 1, LANES * (t % 2) : LANES * (t % 2 + 1)]
                cols = slice(LANES * t, LANES * (t + 1))
                o_ref[0, 1, :, cols] = out[32 * n : 32 * n + 32, 0:LANES] * factor
                o_ref[0, 2, :, cols] = out[32 * n : 32 * n + 32, LANES:BLOCK] * factor

    return pl.pallas_call(
        kernel,
        out_shape=jax.ShapeDtypeStruct((1, 3, 32, BLOCK * count), F32),
        in_specs=[SMEM] + [VMEM] * 9,
        out_specs=VMEM,
        scratch_shapes=[
            pltpu.VMEM((count + 1, 32, BLOCK), F32),
            pltpu.VMEM((64 * count, BLOCK), BF16),
            pltpu.VMEM((64 * count, BLOCK), BF16),
            pltpu.VMEM((64 * count, BLOCK), F32),
            pltpu.VMEM((64 * count, BLOCK), BF16),
            pltpu.VMEM((64 * count, BLOCK), BF16),
            pltpu.VMEM((count, BLOCK), F32),
        ],
        compiler_params=PARAMS,
        cost_estimate=cost(8 << 30, 8 << 20),
        name="filtered",
    )(core, sums, near, away, right, right_inv, left, left_inv, band, mean)


def on_device(slc, pair_index):
    right, right_inv, left, left_inv, band, mean = (jnp.asarray(m) for m in constants())
    blocks = lax.axis_size("rows")
    core = (lax.axis_index("rows") % 2).astype(jnp.int32).reshape(1)
    held = lax.all_to_all(spread_chunks(slc, pair_index), "acq", 0, 0)
    second = lax.all_to_all(pick_chunks(held), "acq", 0, 0)
    near, away = edge_rows(slc, second, core)
    away = lax.ppermute(away, "rows", [(i, i + 1) for i in range(1, blocks - 1, 2)] + [(i + 1, i) for i in range(1, blocks - 1, 2)])
    near = lax.ppermute(near, "rows", [(i, i ^ 1) for i in range(blocks)])
    sums = own_sums(slc, second, band)
    return filtered(sums, near, away, core, right, right_inv, left, left_inv, band, mean)


def solution(mesh):
    return jax.shard_map(
        on_device,
        mesh=mesh,
        in_specs=(P("acq", None, "rows", None), P("acq", None)),
        out_specs=P("acq", None, "rows", None),
        check_vma=False,
    )
```

time: 202 us -> 61.5 us (0.30); the launches traced: 200 us -> 61.2 us
  waiting for transfers between devices: 127 us -> 16.1 us
  blocking collectives: 0 us -> 23.4 us
  other arithmetic: 18.6 us -> 0 us
  between operations: 17.4 us -> 0.11 us
  matrix products: 16.5 us -> 0 us
  local copies, waits for them, and re-layouts: 13.3 us -> 1.91 us
  Pallas kernels: 0 us -> 7.67 us
  starting transfers between devices: 7.24 us -> 11.9 us
    all_gather x1 -> x0, waiting for transfers between devices: 122 us -> none  [on_device(): stacked = lax.all_gather(extended, 'acq', axis=0, tiled=True)]
    all_to_all x0 -> x1, blocking collectives: none -> 23.4 us  [on_device(): held = lax.all_to_all(spread_chunks(slc, pair_index), 'acq', 0, 0)]
    dot_general x16 -> x0, matrix products: 16.5 us -> none  [the longest x8 8.71 us: left_mul(): jnp.einsum('ij,ajbk->aibk', matrix, field, precision=lax.Precision.HIGHEST)]
    all_to_all x0 -> x1, waiting for transfers between devices: none -> 15.1 us  [on_device(): second = lax.all_to_all(pick_chunks(held), 'acq', 0, 0)]
    add x3 -> x0, other arithmetic: 13 us -> none  [the longest x1 10.1 us: boxsum(): result = result + total[..., :, shift:shift + cols_out]]
    pallas_call x0 -> x5, Pallas kernels: none -> 7.67 us  [the longest x1 4.19 us: filtered(): pl.pallas_call(kernel, out_shape=jax.ShapeDtypeStruct((1, 3, 32, BLOCK *...]
    mul x6 -> x0, local copies, waits for them, and re-layouts: 4 us -> none  [the longest x2 1.4 us: pair_terms(): gamma_re = sums[0] * scale]
    all_to_all x0 -> x1, starting transfers between devices: none -> 3.79 us  [on_device(): second = lax.all_to_all(pick_chunks(held), 'acq', 0, 0)]
  transfers between devices with their start and end apart: 3 -> 3, of which waited for: 2 -> 2; matrix products, arithmetic and copies ran while one was open for 0% -> 0% of each run, Pallas kernels for 0% -> 3%
where the time goes in v1:
time: 61.5 us; the launch traced here: 61.2 us
  blocking collectives  23.4 us (38%)
  waiting for transfers between devices  16.1 us (26%)
  starting transfers between devices  11.9 us (19%)
  Pallas kernels  7.67 us (12%)
  local copies, waits for them, and re-layouts  1.91 us (3%)
    all_to_all x1, blocking collectives, on_device(): held = lax.all_to_all(spread_chunks(slc, pair_index), 'acq', 0, 0)  23.4 us
    all_to_all x1, waiting for transfers between devices, on_device(): second = lax.all_to_all(pick_chunks(held), 'acq', 0, 0)  15.1 us
    ppermute x1, starting transfers between devices, on_device(): lax.ppermute(away, 'rows', [(i, i + 1) for i in range(1, blocks - 1, 2)]...  4.83 us
    pallas_call x1, Pallas kernels, filtered(): pl.pallas_call(kernel, out_shape=jax.ShapeDtypeStruct((1, 3, 32, BLOCK *...  4.19 us
    all_to_all x1, starting transfers between devices, on_device(): second = lax.all_to_all(pick_chunks(held), 'acq', 0, 0)  3.79 us
    ppermute x1, starting transfers between devices, on_device(): near = lax.ppermute(near, 'rows', [(i, i ^ 1) for i in range(blocks)])  3.33 us
    unnamed x18, local copies, waits for them, and re-layouts  1.91 us
    pallas_call x1, Pallas kernels, own_sums(): pl.pallas_call(kernel, out_shape=jax.ShapeDtypeStruct((count, 128, BLOCK)...  1.68 us
  transfers between devices with their start and end apart: 3, of which 2 were waited for; matrix products, arithmetic and copies ran while one was open for 0% of the time, Pallas kernels for 3%

profile of v1, /device:TPU:97, one launch (start us, length us, event | category | flops | bytes accessed | tf_op | source)
XLA Modules:
  0.0 61.2 jit_solution(6913146016638548038)
XLA Ops:
  0.0 0.0 copy-start
  0.0 1.2 %copy-done = f32[1,2,32,4096]{3,2,1,0:T(8,128)S(1)} copy-done((f32[1,2,32,4096]{3,2,1,0:T(8,128)S(1)}, f32[1,2,32,4096]{3,2,1,0:T(8,128)}, u32[]{:S(2)}) %copy-start) | copy-done | bytes 1048600
  1.2 0.0 copy-start.2
  1.2 0.7 %copy-done.2 = s32[1,2]{1,0:T(1,128)S(1)} copy-done((s32[1,2]{1,0:T(1,128)S(1)}, s32[1,2]{1,0:T(1,128)}, u32[]{:S(2)}) %copy-start.2) | copy-done | bytes 32
  1.9 0.6 spread_chunks.1
  2.5 23.4 %all_to_all.10.v_ref = f32[16,136,128]{2,1,0:T(8,128)S(1)} all-to-all(f32[16,136,128]{2,1,0:T(8,128)S(1)} %spread_chunks.1), channel_id=1, replica_groups=mesh['acq'=16,'rows'=16] {'acq'}, dimensions={0} | all-to-all | bytes 2228224 | tf_op jit(solution)/shard_map/all_to_all | solution.py:303
  25.9 1.1 %pick_chunks.1 = f32[16,128,128]{2,1,0:T(8,128)} custom-call(f32[16,136,128]{2,1,0:T(8,128)S(1)} %all_to_all.10.v_ref), custom_call_target="tpu_custom_call" | custom-call | bytes 2097152 | tf_op jit(solution)/shard_map/pick_chunks/pallas_call | solution.py:100
  27.0 0.0 copy-start.1
  27.0 3.8 %all-to-all-start.1 = ((f32[16,128,128]{2,1,0:T(8,128)}), f32[16,128,128]{2,1,0:T(8,128)S(1)}, u32[]{:S(2)}, u32[]{:S(2)}) async-start(f32[16,128,128]{2,1,0:T(8,128)} %pick_chunks.1), calls=%async_computation.1 | async-start | bytes 2097152 | tf_op jit(solution)/shard_map/all_to_all | solution.py:304
  30.8 0.0 copy-start.3
  30.8 15.1 %all-to-all-done.1.b_ref = f32[16,128,128]{2,1,0:T(8,128)S(1)} async-done(((f32[16,128,128]{2,1,0:T(8,128)}), f32[16,128,128]{2,1,0:T(8,128)S(1)}, u32[]{:S(2)}, u32[]{:S(2)}) %all-to-all-start.1) | async-done | bytes 1048608 | tf_op jit(solution)/shard_map/all_to_all | solution.py:304
  45.9 0.0 copy-done.1
  45.9 0.1 edge_rows.1
  46.0 3.3 %collective-permute-start = (f32[2,16,8,128]{3,2,1,0:T(8,128)S(1)}, f32[2,16,8,128]{3,2,1,0:T(8,128)S(1)}, u32[]{:S(2)}, u32[]{:S(2)}) collective-permute-start(f32[2,16,8,128]{3,2,1,0:T(8,128)S(1)} %get-tuple-element.7), channel_id=1, source_target_pairs={{0,1},{1,0},{2,3},{3,2},{4,5},{5,4},{6,7},{7,6},{8,9},{9,8},{10,11... | collective-permute-start | bytes 393224 | tf_op jit(solution)/shard_map/ppermute | solution.py:307
  49.3 0.0 copy-start.4
  49.3 0.0 copy-start.5
  49.3 0.0 copy-start.6
  49.3 0.0 copy-start.7
  49.3 0.0 copy-start.8
  49.4 4.8 %collective-permute-start.1 = (f32[2,16,8,128]{3,2,1,0:T(8,128)S(1)}, f32[2,16,8,128]{3,2,1,0:T(8,128)S(1)}, u32[]{:S(2)}, u32[]{:S(2)}) collective-permute-start(f32[2,16,8,128]{3,2,1,0:T(8,128)S(1)} %get-tuple-element.8), channel_id=1, source_target_pairs={{1,2},{3,4},{5,6},{7,8},{9,10},{11,12},{13,14},{2,1},{4,3},{6,5},{... | collective-permute-start | bytes 393224 | tf_op jit(solution)/shard_map/ppermute | solution.py:306
  54.2 0.0 copy-done.3
  54.2 1.7 %own_sums.1.s_ref = f32[16,128,256]{2,1,0:T(8,128)S(1)} custom-call(f32[1,2,32,4096]{3,2,1,0:T(8,128)S(1)} %copy-done.1, f32[16,128,128]{2,1,0:T(8,128)S(1)} %all-to-all-done.1.b_ref, bf16[1024,256]{1,0:T(8,128)(2,1)S(1)} %copy-done.3), custom_call_target="tpu_custom_call" | custom-call | flops 4294967296 | bytes 8388608 | tf_op jit(solution)/shard_map/own_sums/pallas_call | solution.py:174
  55.9 0.0 collective-permute-done.near_ref
  55.9 1.1 %collective-permute-done.1.away_ref = f32[2,16,8,128]{3,2,1,0:T(8,128)S(1)} collective-permute-done((f32[2,16,8,128]{3,2,1,0:T(8,128)S(1)}, f32[2,16,8,128]{3,2,1,0:T(8,128)S(1)}, u32[]{:S(2)}, u32[]{:S(2)}) %collective-permute-start.1) | collective-permute-done | bytes 131104 | tf_op jit(solution)/shard_map/ppermute | solution.py:306
  57.0 0.0 copy-done.4
  57.0 0.0 copy-done.5
  57.0 0.0 copy-done.6
  57.0 0.0 copy-done.7
  57.0 0.0 copy-done.8
  57.0 4.2 %filtered.1 = f32[1,3,32,4096]{3,2,1,0:T(8,128)} custom-call(s32[1]{0:T(128)} %bitcast.core_ref, f32[16,128,256]{2,1,0:T(8,128)S(1)} %own_sums.1.s_ref, f32[2,16,8,128]{3,2,1,0:T(8,128)S(1)} %collective-permute-done.near_ref, f32[2,16,8,128]{3,2,1,0:T(8,128)S(1)} %collective-permute-done.1.away_ref, bf16[768,256]{1,0:T(8,128)(2,1)S(1)} %copy-done.5, ...), custom_call_target="tpu_custom_call" | custom-call | flops 8589934592 | bytes 8388608 | tf_op jit(solution)/shard_map/filtered/pallas_call | solution.py:279
Async XLA Ops:
  0.0 1.2 %copy-start = (f32[1,2,32,4096]{3,2,1,0:T(8,128)S(1)}, f32[1,2,32,4096]{3,2,1,0:T(8,128)}, u32[]{:S(2)}) copy-start(f32[1,2,32,4096]{3,2,1,0:T(8,128)} %a_ref.3) | copy-start | bytes 3145732
  1.2 0.7 %copy-start.2 = (s32[1,2]{1,0:T(1,128)S(1)}, s32[1,2]{1,0:T(1,128)}, u32[]{:S(2)}) copy-start(s32[1,2]{1,0:T(1,128)} %pair_ref.1) | copy-start | bytes 28
  27.0 18.9 %copy-start.1 = (f32[1,2,32,4096]{3,2,1,0:T(8,128)S(1)}, f32[1,2,32,4096]{3,2,1,0:T(8,128)}, u32[]{:S(2)}) copy-start(f32[1,2,32,4096]{3,2,1,0:T(8,128)} %a_ref.3) | copy-start | bytes 3145732
  27.0 18.9 %all-to-all-start.1 = ((f32[16,128,128]{2,1,0:T(8,128)}), f32[16,128,128]{2,1,0:T(8,128)S(1)}, u32[]{:S(2)}, u32[]{:S(2)}) async-start(f32[16,128,128]{2,1,0:T(8,128)} %pick_chunks.1), calls=%async_computation.1 | async-start | bytes 2097152 | tf_op jit(solution)/shard_map/all_to_all | solution.py:304
  30.8 23.4 %copy-start.3 = (bf16[1024,256]{1,0:T(8,128)(2,1)S(1)}, bf16[1024,256]{1,0:T(8,128)(2,1)}, u32[]{:S(2)}) copy-start(bf16[1024,256]{1,0:T(8,128)(2,1)} %constant.33.clone.w_ref) | copy-start | bytes 1572868
  46.0 9.9 %collective-permute-start = (f32[2,16,8,128]{3,2,1,0:T(8,128)S(1)}, f32[2,16,8,128]{3,2,1,0:T(8,128)S(1)}, u32[]{:S(2)}, u32[]{:S(2)}) collective-permute-start(f32[2,16,8,128]{3,2,1,0:T(8,128)S(1)} %get-tuple-element.7), channel_id=1, source_target_pairs={{0,1},{1,0},{2,3},{3,2},{4,5},{5,4},{6,7},{7,6},{8,9},{9,8},{10,11... | collective-permute-start | bytes 393224 | tf_op jit(solution)/shard_map/ppermute | solution.py:307
  49.3 7.7 %copy-start.4 = (bf16[768,256]{1,0:T(8,128)(2,1)S(1)}, bf16[768,256]{1,0:T(8,128)(2,1)}, u32[]{:S(2)}) copy-start(bf16[768,256]{1,0:T(8,128)(2,1)} %constant.30.clone.ri_ref) | copy-start | bytes 1179652
  49.3 7.7 %copy-start.5 = (bf16[768,256]{1,0:T(8,128)(2,1)S(1)}, bf16[768,256]{1,0:T(8,128)(2,1)}, u32[]{:S(2)}) copy-start(bf16[768,256]{1,0:T(8,128)(2,1)} %constant.29.clone.r_ref) | copy-start | bytes 1179652
  49.3 7.7 %copy-start.6 = (bf16[512,256]{1,0:T(8,128)(2,1)S(1)}, bf16[512,256]{1,0:T(8,128)(2,1)}, u32[]{:S(2)}) copy-start(bf16[512,256]{1,0:T(8,128)(2,1)} %constant.34.clone.m_ref) | copy-start | bytes 786436
  49.3 7.7 %copy-start.7 = (bf16[64,192]{1,0:T(8,128)(2,1)S(1)}, bf16[64,192]{1,0:T(8,128)(2,1)}, u32[]{:S(2)}) copy-start(bf16[64,192]{1,0:T(8,128)(2,1)} %constant.32.clone.li_ref) | copy-start | bytes 73732
  49.3 7.7 %copy-start.8 = (bf16[64,192]{1,0:T(8,128)(2,1)S(1)}, bf16[64,192]{1,0:T(8,128)(2,1)}, u32[]{:S(2)}) copy-start(bf16[64,192]{1,0:T(8,128)(2,1)} %constant.31.clone.l_ref) | copy-start | bytes 73732
  49.4 7.6 %collective-permute-start.1 = (f32[2,16,8,128]{3,2,1,0:T(8,128)S(1)}, f32[2,16,8,128]{3,2,1,0:T(8,128)S(1)}, u32[]{:S(2)}, u32[]{:S(2)}) collective-permute-start(f32[2,16,8,128]{3,2,1,0:T(8,128)S(1)} %get-tuple-element.8), channel_id=1, source_target_pairs={{1,2},{3,4},{5,6},{7,8},{9,10},{11,12},{13,14},{2,1},{4,3},{6,5},{... | collective-permute-start | bytes 393224 | tf_op jit(solution)/shard_map/ppermute | solution.py:306

commit v2 on v1

v2 whole, which is shorter than its diff:
```python
import functools

import jax
import jax.numpy as jnp
import ml_dtypes
import numpy as np
from jax import lax
from jax.experimental import pallas as pl
from jax.experimental.pallas import tpu as pltpu
from jax.sharding import PartitionSpec as P

LOOK_R = 5
LOOK_C = 19
PATCH = 32
LANES = 128
BLOCK = 256
OWN_GROUP = 16
LATE_GROUPS = 4
EARLY_GROUPS = 4
EDGE_GROUP = 8
VMEM = pl.BlockSpec(memory_space=pltpu.VMEM)
SMEM = pl.BlockSpec(memory_space=pltpu.SMEM)
PARAMS = pltpu.CompilerParams(vmem_limit_bytes=40 * 1024 * 1024)
F32 = jnp.float32
BF16 = jnp.bfloat16


def cost(flops, moved):
    return pl.CostEstimate(flops=flops, bytes_accessed=moved, transcendentals=0)


def halves(matrix):
    high = matrix.astype(ml_dtypes.bfloat16)
    low = (matrix - high.astype(np.float64)).astype(ml_dtypes.bfloat16)
    return high, low


def split(x):
    high = x.astype(BF16)
    low = (x - high.astype(F32)).astype(BF16)
    return high, low


def constants():
    index = np.arange(PATCH)
    phase = 2.0 * np.pi / PATCH * (index[:, None] * index[None, :] % PATCH)
    c, s = np.cos(phase), np.sin(phase)
    eye = np.eye(LANES // PATCH)
    cb, sb = np.kron(eye, c), np.kron(eye, s)

    def three_rows(m):
        h, l = halves(m)
        return np.concatenate([h, h, l], axis=0)

    def three_cols(m):
        h, l = halves(m)
        return np.concatenate([h, h, l], axis=1)

    right = three_rows(np.block([[cb, -sb], [sb, cb]]))
    right_inv = three_rows(np.block([[cb, sb], [-sb, cb]]) / (PATCH * PATCH))
    left = three_cols(np.block([[c, s], [-s, c]]))
    left_inv = three_cols(np.block([[c, -s], [s, c]]))
    half = LOOK_C // 2
    row, col = np.arange(BLOCK)[:, None], np.arange(BLOCK)[None, :]
    near = (np.abs(row - LANES - col) <= half).astype(ml_dtypes.bfloat16)
    far = (np.abs(row + LANES - col) <= half).astype(ml_dtypes.bfloat16)
    band = np.concatenate([near, near, far, far], axis=0)
    mean = np.kron(np.eye(BLOCK // PATCH), np.full((PATCH, PATCH), 1.0 / (PATCH * PATCH))).astype(ml_dtypes.bfloat16)
    mean = np.concatenate([mean, mean], axis=0)
    return right, right_inv, left, left_inv, band, mean


def spread_chunks(slc, pair_index, core):
    count = slc.shape[3] // BLOCK

    def kernel(core_ref, x_ref, pair_ref, o_ref, wanted_ref, held_ref, pair_sem, in_sem, out_sem):
        pair_copy = pltpu.make_async_copy(pair_ref, wanted_ref, pair_sem)
        pair_copy.start()

        def start(first, last, sem):
            for j in range(first, last):
                for k in range(2):
                    cols = slice(BLOCK * j + LANES * k, BLOCK * j + LANES * (k + 1))
                    for c in range(2):
                        rows = slice(64 * k + 32 * c, 64 * k + 32 * c + 32)
                        pltpu.make_async_copy(x_ref.at[0, c, :, cols], held_ref.at[j, rows], sem).start()

        def wait(first, last, sem):
            part = held_ref.at[first:last, 0:128]
            pltpu.make_async_copy(part, part, sem).wait()

        def out(first, last, sem):
            return pltpu.make_async_copy(held_ref.at[first:last], o_ref.at[first:last], sem)

        def fill():
            pair_copy.wait()
            wanted = jnp.full((8, LANES), wanted_ref[0, 1].astype(F32))
            for j in range(count):
                held_ref[j, 128:136] = wanted

        @pl.when(core_ref[0] == 0)
        def _():
            n = count // LATE_GROUPS
            for g in range(LATE_GROUPS):
                start(g * n, g * n + n, in_sem.at[g])
                if g == 0:
                    fill()
                wait(g * n, g * n + n, in_sem.at[g])
                copy = out(g * n, g * n + n, out_sem.at[g])
                copy.start()
                copy.wait()

        @pl.when(core_ref[0] != 0)
        def _():
            n = count // EARLY_GROUPS
            for g in range(EARLY_GROUPS):
                start(g * n, g * n + n, in_sem.at[g])
            fill()
            copies = [out(g * n, g * n + n, out_sem.at[g]) for g in range(EARLY_GROUPS)]
            for g in range(EARLY_GROUPS):
                wait(g * n, g * n + n, in_sem.at[g])
                copies[g].start()
            for copy in copies:
                copy.wait()

    hbm = pl.BlockSpec(memory_space=pltpu.HBM)
    return pl.pallas_call(
        kernel,
        out_shape=jax.ShapeDtypeStruct((count, 136, LANES), F32),
        in_specs=[SMEM, hbm, hbm],
        out_specs=hbm,
        scratch_shapes=[
            pltpu.SMEM((1, 2), jnp.int32),
            pltpu.VMEM((count, 136, LANES), F32),
            pltpu.SemaphoreType.DMA,
            pltpu.SemaphoreType.DMA((max(LATE_GROUPS, EARLY_GROUPS),)),
            pltpu.SemaphoreType.DMA((max(LATE_GROUPS, EARLY_GROUPS),)),
        ],
        compiler_params=pltpu.CompilerParams(vmem_limit_bytes=60 * 1024 * 1024),
        cost_estimate=cost(0, 2 << 20),
        name="spread_chunks",
    )(core, slc, pair_index)


def pick_chunks(held):
    count = held.shape[0]

    def kernel(v_ref, o_ref):
        for p in range(count):
            wanted = v_ref[p, 128:129, 0:1][0, 0].astype(jnp.int32)
            o_ref[p] = v_ref[wanted, 0:128]

    return pl.pallas_call(
        kernel,
        out_shape=jax.ShapeDtypeStruct((count, 128, LANES), F32),
        in_specs=[VMEM],
        out_specs=VMEM,
        compiler_params=PARAMS,
        cost_estimate=cost(0, 2 << 20),
        name="pick_chunks",
    )(held)


def first_sides(core, top, low):
    return jnp.where(core == 0, low, top), jnp.where(core == 0, top, low)


def edge_rows_first(slc, core):
    count = slc.shape[3] // BLOCK

    def kernel(core_ref, a_ref, near_ref, away_ref):
        for j in range(count):
            for k in range(2):
                cols = slice(BLOCK * j + LANES * k, BLOCK * j + LANES * (k + 1))
                for c in range(2):
                    at = slice(4 * c + 2 * k, 4 * c + 2 * k + 2)
                    near_ref[j, at], away_ref[j, at] = first_sides(
                        core_ref[0], a_ref[0, c, 0:2, cols], a_ref[0, c, 30:32, cols]
                    )

    shape = jax.ShapeDtypeStruct((count, 8, LANES), F32)
    return pl.pallas_call(
        kernel,
        out_shape=(shape, shape),
        in_specs=[SMEM, VMEM],
        out_specs=(VMEM, VMEM),
        compiler_params=PARAMS,
        cost_estimate=cost(0, 1 << 20),
        name="edge_rows_first",
    )(core, slc)


def edge_rows_second(second, core):
    count = second.shape[0]

    def kernel(core_ref, b_ref, near_ref, away_ref):
        for j in range(count):
            for k in range(2):
                for c in range(2):
                    at = slice(4 * c + 2 * k, 4 * c + 2 * k + 2)
                    base = 64 * k + 32 * c
                    near_ref[j, at], away_ref[j, at] = first_sides(
                        core_ref[0], b_ref[j, base : base + 2], b_ref[j, base + 30 : base + 32]
                    )

    shape = jax.ShapeDtypeStruct((count, 8, LANES), F32)
    return pl.pallas_call(
        kernel,
        out_shape=(shape, shape),
        in_specs=[SMEM, VMEM],
        out_specs=(VMEM, VMEM),
        compiler_params=PARAMS,
        cost_estimate=cost(0, 1 << 20),
        name="edge_rows_second",
    )(core, second)


def gamma_of(total):
    scale = lax.rsqrt(total[2] * total[3] + 1e-06)
    gr, gi = total[0] * scale, total[1] * scale
    return gr, gi, jnp.sqrt(gr * gr + gi * gi)


def put_tiles(ref, j, real, imag):
    for k in range(2):
        cols = slice(LANES * k, LANES * (k + 1))
        ref[2 * j + k, :, 0:LANES] = real[:, cols]
        ref[2 * j + k, :, LANES:BLOCK] = imag[:, cols]


def get_tiles(ref, j):
    real = jnp.concatenate([ref[2 * j, :, 0:LANES], ref[2 * j + 1, :, 0:LANES]], axis=1)
    imag = jnp.concatenate([ref[2 * j, :, LANES:BLOCK], ref[2 * j + 1, :, LANES:BLOCK]], axis=1)
    return jnp.concatenate([real, imag], axis=0)


def box_columns(high_ref, low_ref, band, start, n):
    rows = n * high_ref.shape[1]
    parts = [ref[start + d : start + d + n].reshape(rows, BLOCK) for d in range(2) for ref in (high_ref, low_ref)]
    return jnp.dot(jnp.concatenate(parts, axis=1), band, preferred_element_type=F32)


def staggered(count, group, stages):
    starts = list(range(0, count, group))
    for t in range(len(starts) + len(stages) - 1):
        for s in reversed(range(len(stages))):
            if 0 <= t - s < len(starts):
                stages[s](starts[t - s])


def own_part(slc, second, band, right):
    count = second.shape[0]
    group = OWN_GROUP

    def kernel(a_ref, b_ref, w_ref, r_ref, y_ref, edge_ref, coh_ref, rows_ref, high_ref, low_ref, gh_ref, gl_ref):
        zero8 = jnp.zeros((8, LANES), F32)
        for slot in range(8):
            rows_ref[slot, 0:8] = zero8
            rows_ref[slot, 40:48] = zero8
        zero = jnp.zeros((128, LANES), BF16)
        for ref in (high_ref, low_ref):
            ref[0, :, 0:LANES] = zero
            ref[count, :, LANES:BLOCK] = zero
        sub = lax.broadcasted_iota(jnp.int32, (8, BLOCK), 0)
        row = lax.broadcasted_iota(jnp.int32, (32, BLOCK), 0)
        inner = (row >= 2) & (row < 30)

        def row_sums(g):
            for t in range(2 * g + 1 if g else 0, min(2 * (g + group) + 1, 2 * count)):
                j, k = t // 2, t % 2
                cols = slice(LANES * t, LANES * (t + 1))
                a0, a1 = a_ref[0, 0, :, cols], a_ref[0, 1, :, cols]
                b0, b1 = b_ref[j, 64 * k : 64 * k + 32], b_ref[j, 64 * k + 32 : 64 * k + 64]
                fields = (a0 * b0 + a1 * b1, a1 * b0 - a0 * b1, a0 * a0 + a1 * a1, b0 * b0 + b1 * b1)
                at, side = (t + 1) // 2, (t + 1) % 2
                lanes = slice(LANES * side, LANES * (side + 1))
                for f, field in enumerate(fields):
                    slot = 4 * (t % 2) + f
                    rows_ref[slot, 8:40] = field
                    total = field
                    for shift in (6, 7, 9, 10):
                        total = total + rows_ref[slot, shift : shift + 32]
                    high, low = split(total)
                    high_ref[at, 32 * f : 32 * f + 32, lanes] = high
                    low_ref[at, 32 * f : 32 * f + 32, lanes] = low

        def gamma(g):
            sums = box_columns(high_ref, low_ref, w_ref[...], g, group)
            for j in range(g, g + group):
                total = [sums[128 * (j - g) + 32 * f : 128 * (j - g) + 32 * f + 32] for f in range(4)]
                for f in range(4):
                    edge_ref[j, 8 * f : 8 * f + 8] = jnp.where(sub < 4, total[f][0:8], total[f][24:32])
                gr, gi, coherence = gamma_of(total)
                coh_ref[:, BLOCK * j : BLOCK * (j + 1)] = coherence
                gr, gi = jnp.where(inner, gr, 0.0), jnp.where(inner, gi, 0.0)
                rh, rl = split(gr)
                ih, il = split(gi)
                put_tiles(gh_ref, j, rh, ih)
                put_tiles(gl_ref, j, rl, il)

        def transform(g):
            m, n = 2 * g, 2 * group
            h, l = (ref[m : m + n].reshape(32 * n, BLOCK) for ref in (gh_ref, gl_ref))
            y = jnp.dot(jnp.concatenate([h, l, h], axis=1), r_ref[...], preferred_element_type=F32)
            y_ref[m : m + n] = y.reshape(n, 32, BLOCK)

        staggered(count, group, (row_sums, gamma, transform))

    return pl.pallas_call(
        kernel,
        out_shape=(
            jax.ShapeDtypeStruct((2 * count, 32, BLOCK), F32),
            jax.ShapeDtypeStruct((count, 32, BLOCK), F32),
            jax.ShapeDtypeStruct((32, BLOCK * count), F32),
        ),
        in_specs=[VMEM] * 4,
        out_specs=(VMEM, VMEM, VMEM),
        scratch_shapes=[
            pltpu.VMEM((8, 48, LANES), F32),
            pltpu.VMEM((count + 1, 128, BLOCK), BF16),
            pltpu.VMEM((count + 1, 128, BLOCK), BF16),
            pltpu.VMEM((2 * count, 32, BLOCK), BF16),
            pltpu.VMEM((2 * count, 32, BLOCK), BF16),
        ],
        compiler_params=PARAMS,
        cost_estimate=cost(4 << 30, 12 << 20),
        name="own_part",
    )(slc, second, band, right)


def with_edges(half_spectrum, edge_sums, coherence, halos, core, right, right_inv, left, left_inv, band, mean):
    count = edge_sums.shape[0]
    group = EDGE_GROUP

    def kernel(core_ref, yin_ref, edge_ref, coh_ref, an_ref, aw_ref, bn_ref, bw_ref,
               r_ref, ri_ref, l_ref, li_ref, w_ref, m_ref, o_ref,
               part_ref, high_ref, low_ref, g_ref, y_ref, z_ref, vh_ref, vl_ref, strip_ref, out_ref, sem):
        copies = [pltpu.make_async_copy(coh_ref.at[8:24], o_ref.at[0, 0, 8:24], sem.at[0])]
        copies[0].start()
        even = core_ref[0] == 0
        odd_row = lax.broadcasted_iota(jnp.int32, (8, LANES), 0) % 2 == 1
        sub = lax.broadcasted_iota(jnp.int32, (8, BLOCK), 0)
        outer = (sub < 2) | (sub >= 6)
        part_ref[...] = jnp.zeros(part_ref.shape, F32)
        for j in range(count):
            for place in range(2):
                a, b = (
                    jnp.where(even == (place == 1), near[j], away[j])
                    for near, away in ((an_ref, aw_ref), (bn_ref, bw_ref))
                )
                mixed = a * pltpu.roll(b, 4, 0)
                same, aa, bb = a * b, a * a, b * b
                fields = (
                    same + pltpu.roll(same, 4, 0),
                    pltpu.roll(mixed, 4, 0) - mixed,
                    aa + pltpu.roll(aa, 4, 0),
                    bb + pltpu.roll(bb, 4, 0),
                )
                for f, field in enumerate(fields):
                    if place == 0:
                        field = jnp.where(odd_row, field, field + pltpu.roll(field, 7, 0))
                    else:
                        field = jnp.where(odd_row, field + pltpu.roll(field, 1, 0), field)
                    row = 8 * f + 6 * place
                    part_ref[j, row : row + 2, LANES:BLOCK] = field[0:2]
                    part_ref[j + 1, row : row + 2, 0:LANES] = field[2:4]
        for j in range(count + 1):
            high_ref[j], low_ref[j] = split(part_ref[j])

        def gamma(g):
            more = box_columns(high_ref, low_ref, w_ref[...], g, group)
            for j in range(g, g + group):
                at = 32 * (j - g)
                total = [edge_ref[j, 8 * f : 8 * f + 8] + more[at + 8 * f : at + 8 * f + 8] for f in range(4)]
                gr, gi, coherence = gamma_of(total)
                cols = slice(BLOCK * j, BLOCK * (j + 1))
                strip_ref[0, :, cols] = jnp.where(sub < 2, coherence, coh_ref[0:8, cols])
                strip_ref[1, :, cols] = jnp.where(sub >= 6, coherence, coh_ref[24:32, cols])
                put_tiles(g_ref, j, jnp.where(outer, gr, 0.0), jnp.where(outer, gi, 0.0))

        def transform(g):
            m, n = 2 * g, 2 * group
            h, l = split(g_ref[m : m + n].reshape(8 * n, BLOCK))
            y = jnp.dot(jnp.concatenate([h, l, h], axis=1), r_ref[...], preferred_element_type=F32)
            for t in range(n):
                more = y[8 * t : 8 * t + 8]
                y_ref[m + t, 0:8] = yin_ref[m + t, 0:8] + jnp.where(sub < 4, more, 0.0)
                y_ref[m + t, 8:24] = yin_ref[m + t, 8:24]
                y_ref[m + t, 24:32] = yin_ref[m + t, 24:32] + jnp.where(sub < 4, 0.0, more)

        def forward(g):
            for j in range(g, g + group):
                h, l = split(get_tiles(y_ref, j))
                z_ref[j] = jnp.dot(l_ref[...], jnp.concatenate([h, l, h], axis=0), preferred_element_type=F32)

        sums = {}

        def backward(g):
            parts = []
            for j in range(g, g + group):
                zr, zi = z_ref[j, 0:32], z_ref[j, 32:64]
                weight = lax.rsqrt(lax.rsqrt(zr * zr + zi * zi + 1e-06))
                parts.append(weight[0:8] + weight[8:16] + weight[16:24] + weight[24:32])
                h, l = split(jnp.concatenate([zr * weight, zi * weight], axis=0))
                v = jnp.dot(li_ref[...], jnp.concatenate([h, l, h], axis=0), preferred_element_type=F32)
                h, l = split(v)
                put_tiles(vh_ref, j, h[0:32], h[32:64])
                put_tiles(vl_ref, j, l[0:32], l[32:64])
            h, l = split(jnp.concatenate(parts, axis=0))
            total = jnp.dot(jnp.concatenate([h, l], axis=1), m_ref[...], preferred_element_type=F32)
            sums[g] = 1.0 / jnp.sum(total.reshape(group, 8, BLOCK), axis=1, keepdims=True)

        def finish(g):
            m, n = 2 * g, 2 * group
            h, l = (ref[m : m + n].reshape(32 * n, BLOCK) for ref in (vh_ref, vl_ref))
            out = jnp.dot(jnp.concatenate([h, l, h], axis=1), ri_ref[...], preferred_element_type=F32)
            for t in range(n):
                factor = sums[g][t // 2, :, LANES * (t % 2) : LANES * (t % 2 + 1)]
                cols = slice(LANES * (m + t), LANES * (m + t + 1))
                out_ref[0, :, cols] = out[32 * t : 32 * t + 32, 0:LANES] * factor
                out_ref[1, :, cols] = out[32 * t : 32 * t + 32, LANES:BLOCK] * factor
            cols = slice(LANES * m, LANES * (m + n))
            copy = pltpu.make_async_copy(out_ref.at[:, :, cols], o_ref.at[0, 1:3, :, cols], sem.at[3 + g // group])
            copy.start()
            copies.append(copy)
            if g + group == count:
                for i in range(2):
                    copy = pltpu.make_async_copy(strip_ref.at[i], o_ref.at[0, 0, 24 * i : 24 * i + 8], sem.at[1 + i])
                    copy.start()
                    copies.append(copy)

        staggered(count, group, (gamma, transform, forward, backward, finish))
        for copy in copies:
            copy.wait()

    return pl.pallas_call(
        kernel,
        out_shape=jax.ShapeDtypeStruct((1, 3, 32, BLOCK * count), F32),
        in_specs=[SMEM] + [VMEM] * 13,
        out_specs=pl.BlockSpec(memory_space=pltpu.HBM),
        scratch_shapes=[
            pltpu.VMEM((count + 1, 32, BLOCK), F32),
            pltpu.VMEM((count + 1, 32, BLOCK), BF16),
            pltpu.VMEM((count + 1, 32, BLOCK), BF16),
            pltpu.VMEM((2 * count, 8, BLOCK), F32),
            pltpu.VMEM((2 * count, 32, BLOCK), F32),
            pltpu.VMEM((count, 64, BLOCK), F32),
            pltpu.VMEM((2 * count, 32, BLOCK), BF16),
            pltpu.VMEM((2 * count, 32, BLOCK), BF16),
            pltpu.VMEM((2, 8, BLOCK * count), F32),
            pltpu.VMEM((2, 32, BLOCK * count), F32),
            pltpu.SemaphoreType.DMA((3 + count // group,)),
        ],
        compiler_params=PARAMS,
        cost_estimate=cost(8 << 30, 8 << 20),
        name="with_edges",
    )(core, half_spectrum, edge_sums, coherence, *halos, right, right_inv, left, left_inv, band, mean)


def on_device(slc, pair_index):
    right, right_inv, left, left_inv, band, mean = (jnp.asarray(m) for m in constants())
    blocks = lax.axis_size("rows")
    core = (lax.axis_index("rows") % 2).astype(jnp.int32).reshape(1)
    between = range(1, blocks - 1, 2)
    far = [(i, i + 1) for i in between] + [(i + 1, i) for i in between]
    pairs = [(i, i ^ 1) for i in range(blocks)]

    def swap(near, away):
        near = lax.ppermute(near, "rows", pairs)
        return near, lax.ppermute(away, "rows", far)

    held = lax.all_to_all(spread_chunks(slc, pair_index, core), "acq", 0, 0)
    first_halo = swap(*edge_rows_first(slc, core))
    second = lax.all_to_all(pick_chunks(held), "acq", 0, 0)
    second_halo = swap(*edge_rows_second(second, core))
    half_spectrum, edge_sums, coherence = own_part(slc, second, band, right)
    return with_edges(
        half_spectrum, edge_sums, coherence, first_halo + second_halo,
        core, right, right_inv, left, left_inv, band, mean,
    )


def solution(mesh):
    return jax.shard_map(
        on_device,
        mesh=mesh,
        in_specs=(P("acq", None, "rows", None), P("acq", None)),
        out_specs=P("acq", None, "rows", None),
        check_vma=False,
    )
```

time: 61.5 us -> 57.6 us (0.937)
  starting transfers between devices: 11.9 us -> 27.1 us
  waiting for transfers between devices: 16.1 us -> 1.18 us
  blocking collectives: 23.4 us -> 19.3 us
  local copies, waits for them, and re-layouts: 1.91 us -> 0.03 us
  Pallas kernels: 7.67 us -> 9.2 us
    ppermute x2 -> x4, starting transfers between devices: 8.16 us -> 23.3 us  [the longest x2 13.7 us: swap(): near = lax.ppermute(near, 'rows', pairs)]
    all_to_all x1, waiting for transfers between devices: 15.1 us -> 1.16 us  [on_device(): second = lax.all_to_all(pick_chunks(held), 'acq', 0, 0)]
    all_to_all x1, blocking collectives: 23.4 us -> 19.3 us  [on_device(): held = lax.all_to_all(spread_chunks(slc, pair_index, core), 'acq', 0, 0)]
    unnamed x18 -> x14, local copies, waits for them, and re-layouts: 1.91 us -> 0.03 us
    pallas_call x1, Pallas kernels: 0.61 us -> 1.98 us  [spread_chunks(): pl.pallas_call(kernel, out_shape=jax.ShapeDtypeStruct((count, 136, LANES)...]
    ppermute x2 -> x4, waiting for transfers between devices: 1.09 us -> 0.01 us  [the longest x2 0.01 us: swap(): return (near, lax.ppermute(away, 'rows', far))]
    pallas_call x3 -> x4, Pallas kernels: 5.98 us -> 6.15 us  [the longest x1 3.07 us: own_part(): pl.pallas_call(kernel, out_shape=(jax.ShapeDtypeStruct((2 * count, 32, BL...]
  transfers between devices with their start and end apart: 3 -> 5, of which waited for: 2 -> 1; matrix products, arithmetic and copies ran while one was open for 0% -> 0% of each run, Pallas kernels for 3% -> 6%
where the time goes in v2:
time: 57.6 us; the launch traced here: 57 us
  starting transfers between devices  27.1 us (47%)
  blocking collectives  19.3 us (34%)
  Pallas kernels  9.2 us (16%)
  waiting for transfers between devices  1.18 us (2%)
    all_to_all x1, blocking collectives, on_device(): held = lax.all_to_all(spread_chunks(slc, pair_index, core), 'acq', 0, 0)  19.3 us
    ppermute x2, starting transfers between devices, swap(): near = lax.ppermute(near, 'rows', pairs)  13.7 us
    ppermute x2, starting transfers between devices, swap(): return (near, lax.ppermute(away, 'rows', far))  9.61 us
    all_to_all x1, starting transfers between devices, on_device(): second = lax.all_to_all(pick_chunks(held), 'acq', 0, 0)  3.79 us
    pallas_call x1, Pallas kernels, own_part(): pl.pallas_call(kernel, out_shape=(jax.ShapeDtypeStruct((2 * count, 32, BL...  3.07 us
    pallas_call x1, Pallas kernels, with_edges(): pl.pallas_call(kernel, out_shape=jax.ShapeDtypeStruct((1, 3, 32, BLOCK *...  2.96 us
    pallas_call x1, Pallas kernels, spread_chunks(): pl.pallas_call(kernel, out_shape=jax.ShapeDtypeStruct((count, 136, LANES)...  1.98 us
    all_to_all x1, waiting for transfers between devices, on_device(): second = lax.all_to_all(pick_chunks(held), 'acq', 0, 0)  1.16 us
  transfers between devices with their start and end apart: 5, of which 1 were waited for; matrix products, arithmetic and copies ran while one was open for 0% of the time, Pallas kernels for 6%

profile of v2, /device:TPU:97, one launch (start us, length us, event | category | flops | bytes accessed | tf_op | source)
XLA Modules:
  0.0 57.0 jit_solution(14952308691088942905)
XLA Ops:
  0.0 2.0 %spread_chunks.1 = f32[16,136,128]{2,1,0:T(8,128)} custom-call(s32[1]{0:T(128)} %bitcast.core_ref, f32[1,2,32,4096]{3,2,1,0:T(8,128)} %a_ref.3, s32[1,2]{1,0:T(1,128)} %pair_ref.1), custom_call_target="tpu_custom_call" | custom-call | bytes 2097152 | tf_op jit(solution)/shard_map/spread_chunks/pallas_call | solution.py:127
  2.0 19.3 %all_to_all.10.v_ref = f32[16,136,128]{2,1,0:T(8,128)S(1)} all-to-all(f32[16,136,128]{2,1,0:T(8,128)} %spread_chunks.1), channel_id=1, replica_groups=mesh['acq'=16,'rows'=16] {'acq'}, dimensions={0} | all-to-all | bytes 2228224 | tf_op jit(solution)/shard_map/all_to_all | solution.py:472
  21.3 1.1 %pick_chunks.1 = f32[16,128,128]{2,1,0:T(8,128)} custom-call(f32[16,136,128]{2,1,0:T(8,128)S(1)} %all_to_all.10.v_ref), custom_call_target="tpu_custom_call" | custom-call | bytes 2097152 | tf_op jit(solution)/shard_map/pick_chunks/pallas_call | solution.py:153
  22.4 0.0 copy-start
  22.4 3.8 %all-to-all-start.1 = ((f32[16,128,128]{2,1,0:T(8,128)}), f32[16,128,128]{2,1,0:T(8,128)S(1)}, u32[]{:S(2)}, u32[]{:S(2)}) async-start(f32[16,128,128]{2,1,0:T(8,128)} %pick_chunks.1), calls=%async_computation.1 | async-start | bytes 2097152 | tf_op jit(solution)/shard_map/all_to_all | solution.py:474
  26.2 0.0 copy-done
  26.2 0.0 copy-start.1
  26.2 0.0 copy-start.2
  26.2 0.1 edge_rows_first.1
  26.3 6.4 %collective-permute-start = (f32[16,8,128]{2,1,0:T(8,128)S(1)}, f32[16,8,128]{2,1,0:T(8,128)S(1)}, u32[]{:S(2)}, u32[]{:S(2)}) collective-permute-start(f32[16,8,128]{2,1,0:T(8,128)S(1)} %get-tuple-element.15), channel_id=1, source_target_pairs={{0,1},{1,0},{2,3},{3,2},{4,5},{5,4},{6,7},{7,6},{8,9},{9,8},{10,11... | collective-permute-start | bytes 196616 | tf_op jit(solution)/shard_map/ppermute | solution.py:469
  32.7 4.8 %collective-permute-start.1 = (f32[16,8,128]{2,1,0:T(8,128)S(1)}, f32[16,8,128]{2,1,0:T(8,128)S(1)}, u32[]{:S(2)}, u32[]{:S(2)}) collective-permute-start(f32[16,8,128]{2,1,0:T(8,128)S(1)} %get-tuple-element.16), channel_id=1, source_target_pairs={{1,2},{3,4},{5,6},{7,8},{9,10},{11,12},{13,14},{2,1},{4,3},{6,5},{... | collective-permute-start | bytes 196616 | tf_op jit(solution)/shard_map/ppermute | solution.py:470
  37.5 1.2 %all-to-all-done.1.b_ref = f32[16,128,128]{2,1,0:T(8,128)S(1)} async-done(((f32[16,128,128]{2,1,0:T(8,128)}), f32[16,128,128]{2,1,0:T(8,128)S(1)}, u32[]{:S(2)}, u32[]{:S(2)}) %all-to-all-start.1) | async-done | bytes 1048608 | tf_op jit(solution)/shard_map/all_to_all | solution.py:474
  38.8 7.2 %collective-permute-start.2 = (f32[16,8,128]{2,1,0:T(8,128)S(1)}, f32[16,8,128]{2,1,0:T(8,128)S(1)}, u32[]{:S(2)}, u32[]{:S(2)}) collective-permute-start(f32[16,8,128]{2,1,0:T(8,128)S(1)} %get-tuple-element.17), channel_id=1, source_target_pairs={{0,1},{1,0},{2,3},{3,2},{4,5},{5,4},{6,7},{7,6},{8,9},{9,8},{10,11... | collective-permute-start | bytes 196616 | tf_op jit(solution)/shard_map/ppermute | solution.py:469
  46.0 0.0 copy-start.3
  46.0 0.0 copy-start.4
  46.0 0.0 copy-start.5
  46.0 0.0 copy-start.6
  46.0 4.8 %collective-permute-start.3 = (f32[16,8,128]{2,1,0:T(8,128)S(1)}, f32[16,8,128]{2,1,0:T(8,128)S(1)}, u32[]{:S(2)}, u32[]{:S(2)}) collective-permute-start(f32[16,8,128]{2,1,0:T(8,128)S(1)} %get-tuple-element.18), channel_id=1, source_target_pairs={{1,2},{3,4},{5,6},{7,8},{9,10},{11,12},{13,14},{2,1},{4,3},{6,5},{... | collective-permute-start | bytes 196616 | tf_op jit(solution)/shard_map/ppermute | solution.py:470
  50.8 0.0 copy-done.1
  50.9 0.0 copy-done.2
  50.9 3.1 %own_part.1 = (f32[32,32,256]{2,1,0:T(8,128)S(1)}, f32[16,32,256]{2,1,0:T(8,128)S(1)}, f32[32,4096]{1,0:T(8,128)S(1)}) custom-call(f32[1,2,32,4096]{3,2,1,0:T(8,128)S(1)} %copy-done, f32[16,128,128]{2,1,0:T(8,128)S(1)} %all-to-all-done.1.b_ref, bf16[1024,256]{1,0:T(8,128)(2,1)S(1)} %copy-done.1, bf16[768,256]{1,0:T(8,128)(2,1)S(1)} %copy-done.2), custom_call_target="tpu_custom_call" | custom-call | flops 4294967296 | bytes 12582912 | tf_op jit(solution)/shard_map/own_part/pallas_call | solution.py:309
  53.9 0.0 collective-permute-done.an_ref
  53.9 0.0 collective-permute-done.1.aw_ref
  54.0 0.0 collective-permute-done.2.bn_ref
  54.0 0.0 collective-permute-done.3.bw_ref
  54.0 0.0 copy-done.3
  54.0 0.0 copy-done.4
  54.0 0.0 copy-done.5
  54.0 0.0 copy-done.6
  54.0 3.0 %with_edges.1 = f32[1,3,32,4096]{3,2,1,0:T(8,128)} custom-call(s32[1]{0:T(128)} %bitcast.core_ref, f32[32,32,256]{2,1,0:T(8,128)S(1)} %get-tuple-element.12.yin_ref, f32[16,32,256]{2,1,0:T(8,128)S(1)} %get-tuple-element.13.edge_ref, f32[32,4096]{1,0:T(8,128)S(1)} %get-tuple-element.14.coh_ref, f32[16,8,128]{2,1,0:T(8,128)S(1)} %collective-permute-done.an_ref, ...), custom_call_target="tpu_custom_call" | custom-call | flops 8589934592 | bytes 8388608 | tf_op jit(solution)/shard_map/with_edges/pallas_call | solution.py:436
  (1 shorter events, 0.0 us)
Async XLA Ops:
  22.4 3.8 %copy-start = (f32[1,2,32,4096]{3,2,1,0:T(8,128)S(1)}, f32[1,2,32,4096]{3,2,1,0:T(8,128)}, u32[]{:S(2)}) copy-start(f32[1,2,32,4096]{3,2,1,0:T(8,128)} %a_ref.3) | copy-start | bytes 3145732
  22.4 16.3 %all-to-all-start.1 = ((f32[16,128,128]{2,1,0:T(8,128)}), f32[16,128,128]{2,1,0:T(8,128)S(1)}, u32[]{:S(2)}, u32[]{:S(2)}) async-start(f32[16,128,128]{2,1,0:T(8,128)} %pick_chunks.1), calls=%async_computation.1 | async-start | bytes 2097152 | tf_op jit(solution)/shard_map/all_to_all | solution.py:474
  26.2 24.6 %copy-start.1 = (bf16[1024,256]{1,0:T(8,128)(2,1)S(1)}, bf16[1024,256]{1,0:T(8,128)(2,1)}, u32[]{:S(2)}) copy-start(bf16[1024,256]{1,0:T(8,128)(2,1)} %constant.33.clone.w_ref) | copy-start | bytes 1572868
  26.2 24.6 %copy-start.2 = (bf16[768,256]{1,0:T(8,128)(2,1)S(1)}, bf16[768,256]{1,0:T(8,128)(2,1)}, u32[]{:S(2)}) copy-start(bf16[768,256]{1,0:T(8,128)(2,1)} %constant.29.clone.r_ref) | copy-start | bytes 1179652
  26.3 27.6 %collective-permute-start = (f32[16,8,128]{2,1,0:T(8,128)S(1)}, f32[16,8,128]{2,1,0:T(8,128)S(1)}, u32[]{:S(2)}, u32[]{:S(2)}) collective-permute-start(f32[16,8,128]{2,1,0:T(8,128)S(1)} %get-tuple-element.15), channel_id=1, source_target_pairs={{0,1},{1,0},{2,3},{3,2},{4,5},{5,4},{6,7},{7,6},{8,9},{9,8},{10,11... | collective-permute-start | bytes 196616 | tf_op jit(solution)/shard_map/ppermute | solution.py:469
  32.7 21.2 %collective-permute-start.1 = (f32[16,8,128]{2,1,0:T(8,128)S(1)}, f32[16,8,128]{2,1,0:T(8,128)S(1)}, u32[]{:S(2)}, u32[]{:S(2)}) collective-permute-start(f32[16,8,128]{2,1,0:T(8,128)S(1)} %get-tuple-element.16), channel_id=1, source_target_pairs={{1,2},{3,4},{5,6},{7,8},{9,10},{11,12},{13,14},{2,1},{4,3},{6,5},{... | collective-permute-start | bytes 196616 | tf_op jit(solution)/shard_map/ppermute | solution.py:470
  38.8 15.2 %collective-permute-start.2 = (f32[16,8,128]{2,1,0:T(8,128)S(1)}, f32[16,8,128]{2,1,0:T(8,128)S(1)}, u32[]{:S(2)}, u32[]{:S(2)}) collective-permute-start(f32[16,8,128]{2,1,0:T(8,128)S(1)} %get-tuple-element.17), channel_id=1, source_target_pairs={{0,1},{1,0},{2,3},{3,2},{4,5},{5,4},{6,7},{7,6},{8,9},{9,8},{10,11... | collective-permute-start | bytes 196616 | tf_op jit(solution)/shard_map/ppermute | solution.py:469
  46.0 8.0 %copy-start.3 = (bf16[768,256]{1,0:T(8,128)(2,1)S(1)}, bf16[768,256]{1,0:T(8,128)(2,1)}, u32[]{:S(2)}) copy-start(bf16[768,256]{1,0:T(8,128)(2,1)} %constant.30.clone.ri_ref) | copy-start | bytes 1179652
  46.0 8.0 %copy-start.4 = (bf16[512,256]{1,0:T(8,128)(2,1)S(1)}, bf16[512,256]{1,0:T(8,128)(2,1)}, u32[]{:S(2)}) copy-start(bf16[512,256]{1,0:T(8,128)(2,1)} %constant.34.clone.m_ref) | copy-start | bytes 786436
  46.0 8.0 %copy-start.5 = (bf16[64,192]{1,0:T(8,128)(2,1)S(1)}, bf16[64,192]{1,0:T(8,128)(2,1)}, u32[]{:S(2)}) copy-start(bf16[64,192]{1,0:T(8,128)(2,1)} %constant.32.clone.li_ref) | copy-start | bytes 73732
  46.0 8.0 %copy-start.6 = (bf16[64,192]{1,0:T(8,128)(2,1)S(1)}, bf16[64,192]{1,0:T(8,128)(2,1)}, u32[]{:S(2)}) copy-start(bf16[64,192]{1,0:T(8,128)(2,1)} %constant.31.clone.l_ref) | copy-start | bytes 73732
  46.0 8.0 %collective-permute-start.3 = (f32[16,8,128]{2,1,0:T(8,128)S(1)}, f32[16,8,128]{2,1,0:T(8,128)S(1)}, u32[]{:S(2)}, u32[]{:S(2)}) collective-permute-start(f32[16,8,128]{2,1,0:T(8,128)S(1)} %get-tuple-element.18), channel_id=1, source_target_pairs={{1,2},{3,4},{5,6},{7,8},{9,10},{11,12},{13,14},{2,1},{4,3},{6,5},{... | collective-permute-start | bytes 196616 | tf_op jit(solution)/shard_map/ppermute | solution.py:470

commit v3 on v2

--- a/solution.py
+++ b/solution.py
@@ -18,6 +18,7 @@
 LATE_GROUPS = 4
 EARLY_GROUPS = 4
 EDGE_GROUP = 8
+OUT_TILES = 4
 VMEM = pl.BlockSpec(memory_space=pltpu.VMEM)
 SMEM = pl.BlockSpec(memory_space=pltpu.SMEM)
 PARAMS = pltpu.CompilerParams(vmem_limit_bytes=40 * 1024 * 1024)
@@ -165,54 +166,29 @@
     return jnp.where(core == 0, low, top), jnp.where(core == 0, top, low)
 
 
-def edge_rows_first(slc, core):
-    count = slc.shape[3] // BLOCK
-
-    def kernel(core_ref, a_ref, near_ref, away_ref):
+def edge_rows(slc, second, core, mark, near):
+    count = second.shape[0]
+
+    def kernel(core_ref, a_ref, b_ref, mark_ref, o_ref):
+        pick = 0 if near else 1
         for j in range(count):
             for k in range(2):
                 cols = slice(BLOCK * j + LANES * k, BLOCK * j + LANES * (k + 1))
                 for c in range(2):
                     at = slice(4 * c + 2 * k, 4 * c + 2 * k + 2)
-                    near_ref[j, at], away_ref[j, at] = first_sides(
-                        core_ref[0], a_ref[0, c, 0:2, cols], a_ref[0, c, 30:32, cols]
-                    )
-
-    shape = jax.ShapeDtypeStruct((count, 8, LANES), F32)
+                    base = 64 * k + 32 * c
+                    o_ref[0, j, at] = first_sides(core_ref[0], a_ref[0, c, 0:2, cols], a_ref[0, c, 30:32, cols])[pick]
+                    o_ref[1, j, at] = first_sides(core_ref[0], b_ref[j, base : base + 2], b_ref[j, base + 30 : base + 32])[pick]
+
     return pl.pallas_call(
         kernel,
-        out_shape=(shape, shape),
-        in_specs=[SMEM, VMEM],
-        out_specs=(VMEM, VMEM),
+        out_shape=jax.ShapeDtypeStruct((2, count, 8, LANES), F32),
+        in_specs=[SMEM, VMEM, VMEM, VMEM],
+        out_specs=VMEM,
         compiler_params=PARAMS,
         cost_estimate=cost(0, 1 << 20),
-        name="edge_rows_first",
-    )(core, slc)
-
-
-def edge_rows_second(second, core):
-    count = second.shape[0]
-
-    def kernel(core_ref, b_ref, near_ref, away_ref):
-        for j in range(count):
-            for k in range(2):
-                for c in range(2):
-                    at = slice(4 * c + 2 * k, 4 * c + 2 * k + 2)
-                    base = 64 * k + 32 * c
-                    near_ref[j, at], away_ref[j, at] = first_sides(
-                        core_ref[0], b_ref[j, base : base + 2], b_ref[j, base + 30 : base + 32]
-                    )
-
-    shape = jax.ShapeDtypeStruct((count, 8, LANES), F32)
-    return pl.pallas_call(
-        kernel,
-        out_shape=(shape, shape),
-        in_specs=[SMEM, VMEM],
-        out_specs=(VMEM, VMEM),
-        compiler_params=PARAMS,
-        cost_estimate=cost(0, 1 << 20),
-        name="edge_rows_second",
-    )(core, second)
+        name="edge_rows_near" if near else "edge_rows_away",
+    )(core, slc, second, mark)
 
 
 def gamma_of(total):
@@ -248,11 +224,18 @@
                 stages[s](starts[t - s])
 
 
-def own_part(slc, second, band, right):
+def own_part(slc, second, core, turn, band, right):
     count = second.shape[0]
     group = OWN_GROUP
 
-    def kernel(a_ref, b_ref, w_ref, r_ref, y_ref, edge_ref, coh_ref, rows_ref, high_ref, low_ref, gh_ref, gl_ref):
+    def kernel(core_ref, a_ref, b_ref, w_ref, r_ref, y_ref, edge_ref, coh_ref, mark_ref, *scratch):
+        mark_ref[...] = jnp.zeros(mark_ref.shape, F32)
+
+        @pl.when(core_ref[0] == turn)
+        def _():
+            work(a_ref, b_ref, w_ref, r_ref, y_ref, edge_ref, coh_ref, *scratch)
+
+    def work(a_ref, b_ref, w_ref, r_ref, y_ref, edge_ref, coh_ref, rows_ref, high_ref, low_ref, gh_ref, gl_ref):
         zero8 = jnp.zeros((8, LANES), F32)
         for slot in range(8):
             rows_ref[slot, 0:8] = zero8
@@ -312,9 +295,10 @@
             jax.ShapeDtypeStruct((2 * count, 32, BLOCK), F32),
             jax.ShapeDtypeStruct((count, 32, BLOCK), F32),
             jax.ShapeDtypeStruct((32, BLOCK * count), F32),
+            jax.ShapeDtypeStruct((8, LANES), F32),
         ),
-        in_specs=[VMEM] * 4,
-        out_specs=(VMEM, VMEM, VMEM),
+        in_specs=[SMEM] + [VMEM] * 4,
+        out_specs=(VMEM, VMEM, VMEM, VMEM),
         scratch_shapes=[
             pltpu.VMEM((8, 48, LANES), F32),
             pltpu.VMEM((count + 1, 128, BLOCK), BF16),
@@ -325,19 +309,27 @@
         compiler_params=PARAMS,
         cost_estimate=cost(4 << 30, 12 << 20),
         name="own_part",
-    )(slc, second, band, right)
-
-
-def with_edges(half_spectrum, edge_sums, coherence, halos, core, right, right_inv, left, left_inv, band, mean):
-    count = edge_sums.shape[0]
+    )(core, slc, second, band, right)
+
+
+def with_edges(late, early, halos, core, right, right_inv, left, left_inv, band, mean):
+    count = late[1].shape[0]
     group = EDGE_GROUP
 
-    def kernel(core_ref, yin_ref, edge_ref, coh_ref, an_ref, aw_ref, bn_ref, bw_ref,
-               r_ref, ri_ref, l_ref, li_ref, w_ref, m_ref, o_ref,
-               part_ref, high_ref, low_ref, g_ref, y_ref, z_ref, vh_ref, vl_ref, strip_ref, out_ref, sem):
+    def kernel(core_ref, *refs):
+        @pl.when(core_ref[0] == 0)
+        def _():
+            work(True, *refs[0:3], *refs[6:])
+
+        @pl.when(core_ref[0] != 0)
+        def _():
+            work(False, *refs[3:])
+
+    def work(even, yin_ref, edge_ref, coh_ref, near_ref, away_ref,
+             r_ref, ri_ref, l_ref, li_ref, w_ref, m_ref, o_ref,
+             part_ref, high_ref, low_ref, g_ref, y_ref, z_ref, vh_ref, vl_ref, strip_ref, out_ref, sem):
         copies = [pltpu.make_async_copy(coh_ref.at[8:24], o_ref.at[0, 0, 8:24], sem.at[0])]
         copies[0].start()
-        even = core_ref[0] == 0
         odd_row = lax.broadcasted_iota(jnp.int32, (8, LANES), 0) % 2 == 1
         sub = lax.broadcasted_iota(jnp.int32, (8, BLOCK), 0)
         outer = (sub < 2) | (sub >= 6)
@@ -345,8 +337,8 @@
         for j in range(count):
             for place in range(2):
                 a, b = (
-                    jnp.where(even == (place == 1), near[j], away[j])
-                    for near, away in ((an_ref, aw_ref), (bn_ref, bw_ref))
+                    near_ref[i, j] if even == (place == 1) else away_ref[i, j]
+                    for i in range(2)
                 )
                 mixed = a * pltpu.roll(b, 4, 0)
                 same, aa, bb = a * b, a * a, b * b
@@ -419,10 +411,12 @@
                 cols = slice(LANES * (m + t), LANES * (m + t + 1))
                 out_ref[0, :, cols] = out[32 * t : 32 * t + 32, 0:LANES] * factor
                 out_ref[1, :, cols] = out[32 * t : 32 * t + 32, LANES:BLOCK] * factor
-            cols = slice(LANES * m, LANES * (m + n))
-            copy = pltpu.make_async_copy(out_ref.at[:, :, cols], o_ref.at[0, 1:3, :, cols], sem.at[3 + g // group])
-            copy.start()
-            copies.append(copy)
+                if (t + 1) % OUT_TILES == 0:
+                    cols = slice(LANES * (m + t + 1 - OUT_TILES), LANES * (m + t + 1))
+                    at = sem.at[3 + (m + t) // OUT_TILES]
+                    copy = pltpu.make_async_copy(out_ref.at[:, :, cols], o_ref.at[0, 1:3, :, cols], at)
+                    copy.start()
+                    copies.append(copy)
             if g + group == count:
                 for i in range(2):
                     copy = pltpu.make_async_copy(strip_ref.at[i], o_ref.at[0, 0, 24 * i : 24 * i + 8], sem.at[1 + i])
@@ -436,7 +430,7 @@
     return pl.pallas_call(
         kernel,
         out_shape=jax.ShapeDtypeStruct((1, 3, 32, BLOCK * count), F32),
-        in_specs=[SMEM] + [VMEM] * 13,
+        in_specs=[SMEM] + [VMEM] * 14,
         out_specs=pl.BlockSpec(memory_space=pltpu.HBM),
         scratch_shapes=[
             pltpu.VMEM((count + 1, 32, BLOCK), F32),
@@ -449,12 +443,12 @@
             pltpu.VMEM((2 * count, 32, BLOCK), BF16),
             pltpu.VMEM((2, 8, BLOCK * count), F32),
             pltpu.VMEM((2, 32, BLOCK * count), F32),
-            pltpu.SemaphoreType.DMA((3 + count // group,)),
+            pltpu.SemaphoreType.DMA((3 + 2 * count // OUT_TILES,)),
         ],
         compiler_params=PARAMS,
         cost_estimate=cost(8 << 30, 8 << 20),
         name="with_edges",
-    )(core, half_spectrum, edge_sums, coherence, *halos, right, right_inv, left, left_inv, band, mean)
+    )(core, *late, *early, *halos, right, right_inv, left, left_inv, band, mean)
 
 
 def on_device(slc, pair_index):
@@ -465,18 +459,14 @@
     far = [(i, i + 1) for i in between] + [(i + 1, i) for i in between]
     pairs = [(i, i ^ 1) for i in range(blocks)]
 
-    def swap(near, away):
-        near = lax.ppermute(near, "rows", pairs)
-        return near, lax.ppermute(away, "rows", far)
-
     held = lax.all_to_all(spread_chunks(slc, pair_index, core), "acq", 0, 0)
-    first_halo = swap(*edge_rows_first(slc, core))
     second = lax.all_to_all(pick_chunks(held), "acq", 0, 0)
-    second_halo = swap(*edge_rows_second(second, core))
-    half_spectrum, edge_sums, coherence = own_part(slc, second, band, right)
+    *early, mark = own_part(slc, second, core, 1, band, right)
+    away = lax.ppermute(edge_rows(slc, second, core, mark, False), "rows", far)
+    *late, mark = own_part(slc, second, core, 0, band, right)
+    near = lax.ppermute(edge_rows(slc, second, core, mark, True), "rows", pairs)
     return with_edges(
-        half_spectrum, edge_sums, coherence, first_halo + second_halo,
-        core, right, right_inv, left, left_inv, band, mean,
+        late, early, (near, away), core, right, right_inv, left, left_inv, band, mean,
     )
 
 

time: 57.6 us -> 55.1 us (0.957)
  starting transfers between devices: 27.1 us -> 9.55 us
  blocking collectives: 19.3 us -> 34.4 us
  waiting for transfers between devices: 1.18 us -> 2.05 us
  Pallas kernels: 9.2 us -> 8.39 us
    all_to_all x0 -> x1, blocking collectives: none -> 15.1 us  [on_device(): second = lax.all_to_all(pick_chunks(held), 'acq', 0, 0)]
    ppermute x4 -> x2, starting transfers between devices: 23.3 us -> 9.55 us  [the longest x1 9.12 us: on_device(): away = lax.ppermute(edge_rows(slc, second, core, mark, False), 'rows', far)]
    all_to_all x1 -> x0, starting transfers between devices: 3.79 us -> none  [on_device(): second = lax.all_to_all(pick_chunks(held), 'acq', 0, 0)]
    ppermute x4 -> x2, waiting for transfers between devices: 0.01 us -> 2.05 us  [the longest x1 2.05 us: on_device(): away = lax.ppermute(edge_rows(slc, second, core, mark, False), 'rows', far)]
    all_to_all x1 -> x0, waiting for transfers between devices: 1.16 us -> none  [on_device(): second = lax.all_to_all(pick_chunks(held), 'acq', 0, 0)]
    pallas_call x1, Pallas kernels: 1.08 us -> 0.11 us  [pick_chunks(): pl.pallas_call(kernel, out_shape=jax.ShapeDtypeStruct((count, 128, LANES)...]
    pallas_call x1 -> x2, Pallas kernels: 3.07 us -> 3.09 us  [own_part(): pl.pallas_call(kernel, out_shape=(jax.ShapeDtypeStruct((2 * count, 32, BL...]
  transfers between devices with their start and end apart: 5 -> 2, of which waited for: 1 -> 1; matrix products, arithmetic and copies ran while one was open for 0% -> 0% of each run, Pallas kernels for 6% -> 0%
where the time goes in v3:
time: 55.1 us; the launch traced here: 54.6 us
  blocking collectives  34.4 us (62%)
  starting transfers between devices  9.55 us (17%)
  Pallas kernels  8.39 us (15%)
  waiting for transfers between devices  2.05 us (4%)
    all_to_all x1, blocking collectives, on_device(): held = lax.all_to_all(spread_chunks(slc, pair_index, core), 'acq', 0, 0)  19.3 us
    all_to_all x1, blocking collectives, on_device(): second = lax.all_to_all(pick_chunks(held), 'acq', 0, 0)  15.1 us
    ppermute x1, starting transfers between devices, on_device(): away = lax.ppermute(edge_rows(slc, second, core, mark, False), 'rows', far)  9.12 us
    pallas_call x2, Pallas kernels, own_part(): pl.pallas_call(kernel, out_shape=(jax.ShapeDtypeStruct((2 * count, 32, BL...  3.09 us
    pallas_call x1, Pallas kernels, with_edges(): pl.pallas_call(kernel, out_shape=jax.ShapeDtypeStruct((1, 3, 32, BLOCK *...  3.04 us
    ppermute x1, waiting for transfers between devices, on_device(): away = lax.ppermute(edge_rows(slc, second, core, mark, False), 'rows', far)  2.05 us
    pallas_call x1, Pallas kernels, spread_chunks(): pl.pallas_call(kernel, out_shape=jax.ShapeDtypeStruct((count, 136, LANES)...  1.98 us
  transfers between devices with their start and end apart: 2, of which 1 were waited for; matrix products, arithmetic and copies ran while one was open for 0% of the time, Pallas kernels for 0%

profile of v3, /device:TPU:97, one launch (start us, length us, event | category | flops | bytes accessed | tf_op | source)
XLA Modules:
  0.0 54.6 jit_solution(12711136626551868104)
XLA Ops:
  0.0 2.0 %spread_chunks.1 = f32[16,136,128]{2,1,0:T(8,128)} custom-call(s32[1]{0:T(128)} %bitcast.core_ref, f32[1,2,32,4096]{3,2,1,0:T(8,128)} %a_ref.7, s32[1,2]{1,0:T(1,128)} %pair_ref.1), custom_call_target="tpu_custom_call" | custom-call | bytes 2097152 | tf_op jit(solution)/shard_map/spread_chunks/pallas_call | solution.py:128
  2.0 19.3 %all_to_all.10.v_ref = f32[16,136,128]{2,1,0:T(8,128)S(1)} all-to-all(f32[16,136,128]{2,1,0:T(8,128)} %spread_chunks.1), channel_id=1, replica_groups=mesh['acq'=16,'rows'=16] {'acq'}, dimensions={0} | all-to-all | bytes 2228224 | tf_op jit(solution)/shard_map/all_to_all | solution.py:462
  21.3 0.1 pick_chunks.1
  21.4 0.0 copy-start
  21.4 0.0 copy-start.1
  21.5 0.0 copy-start.2
  21.5 15.1 %all_to_all.11.b_ref = f32[16,128,128]{2,1,0:T(8,128)S(1)} all-to-all(f32[16,128,128]{2,1,0:T(8,128)S(1)} %pick_chunks.1), channel_id=1, replica_groups=mesh['acq'=16,'rows'=16] {'acq'}, dimensions={0} | all-to-all | bytes 2097152 | tf_op jit(solution)/shard_map/all_to_all | solution.py:463
  36.5 0.0 copy-done
  36.6 0.0 copy-done.1
  36.6 0.0 copy-done.2
  36.6 3.1 %own_part.3 = (f32[32,32,256]{2,1,0:T(8,128)S(1)}, f32[16,32,256]{2,1,0:T(8,128)S(1)}, f32[32,4096]{1,0:T(8,128)S(1)}, f32[8,128]{1,0:T(8,128)S(1)}) custom-call(s32[1]{0:T(128)} %bitcast.core_ref, f32[1,2,32,4096]{3,2,1,0:T(8,128)S(1)} %copy-done, f32[16,128,128]{2,1,0:T(8,128)S(1)} %all_to_all.11.b_ref, bf16[1024,256]{1,0:T(8,128)(2,1)S(1)} %copy-done.1, ...), custom_call_target="tpu_custom_call" | custom-call | flops 4294967296 | bytes 12582912 | tf_op jit(solution)/shard_map/own_part/pallas_call | solution.py:292
  39.6 0.1 edge_rows_away.1
  39.7 9.1 %collective-permute-start.1 = (f32[2,16,8,128]{3,2,1,0:T(8,128)S(1)}, f32[2,16,8,128]{3,2,1,0:T(8,128)S(1)}, u32[]{:S(2)}, u32[]{:S(2)}) collective-permute-start(f32[2,16,8,128]{3,2,1,0:T(8,128)S(1)} %edge_rows_away.1), channel_id=1, source_target_pairs={{1,2},{3,4},{5,6},{7,8},{9,10},{11,12},{13,14},{2,1},{4,3},{6,5},{... | collective-permute-start | bytes 393224 | tf_op jit(solution)/shard_map/ppermute | solution.py:465
  48.9 0.0 copy-start.3
  48.9 0.0 copy-start.4
  48.9 0.0 copy-start.5
  48.9 0.0 copy-start.6
  48.9 0.1 edge_rows_near.1
  49.0 0.4 collective-permute-start
  49.5 2.0 %collective-permute-done.1.refs_7_ = f32[2,16,8,128]{3,2,1,0:T(8,128)S(1)} collective-permute-done((f32[2,16,8,128]{3,2,1,0:T(8,128)S(1)}, f32[2,16,8,128]{3,2,1,0:T(8,128)S(1)}, u32[]{:S(2)}, u32[]{:S(2)}) %collective-permute-start.1) | collective-permute-done | bytes 131104 | tf_op jit(solution)/shard_map/ppermute | solution.py:465
  51.5 0.0 collective-permute-done.refs_6_
  51.5 0.0 copy-done.3
  51.5 0.0 copy-done.4
  51.5 0.0 copy-done.5
  51.5 0.0 copy-done.6
  51.5 3.0 %with_edges.1 = f32[1,3,32,4096]{3,2,1,0:T(8,128)} custom-call(s32[1]{0:T(128)} %bitcast.core_ref, f32[32,32,256]{2,1,0:T(8,128)S(1)} %get-tuple-element.13.refs_0_, f32[16,32,256]{2,1,0:T(8,128)S(1)} %get-tuple-element.14.refs_1_, f32[32,4096]{1,0:T(8,128)S(1)} %get-tuple-element.15.refs_2_, f32[32,32,256]{2,1,0:T(8,128)S(1)} %get-tuple-element.16.refs_3_, ...), custom_call_target="tpu_custom_call" | custom-call | flops 8589934592 | bytes 8388608 | tf_op jit(solution)/shard_map/with_edges/pallas_call | solution.py:430
  (1 shorter events, 0.0 us)
Async XLA Ops:
  21.4 15.1 %copy-start = (f32[1,2,32,4096]{3,2,1,0:T(8,128)S(1)}, f32[1,2,32,4096]{3,2,1,0:T(8,128)}, u32[]{:S(2)}) copy-start(f32[1,2,32,4096]{3,2,1,0:T(8,128)} %a_ref.7) | copy-start | bytes 3145732
  21.4 15.1 %copy-start.1 = (bf16[1024,256]{1,0:T(8,128)(2,1)S(1)}, bf16[1024,256]{1,0:T(8,128)(2,1)}, u32[]{:S(2)}) copy-start(bf16[1024,256]{1,0:T(8,128)(2,1)} %constant.33.clone.w_ref.refs_12_) | copy-start | bytes 1572868
  21.5 15.1 %copy-start.2 = (bf16[768,256]{1,0:T(8,128)(2,1)S(1)}, bf16[768,256]{1,0:T(8,128)(2,1)}, u32[]{:S(2)}) copy-start(bf16[768,256]{1,0:T(8,128)(2,1)} %constant.29.clone.r_ref.refs_8_) | copy-start | bytes 1179652
  39.7 11.8 %collective-permute-start.1 = (f32[2,16,8,128]{3,2,1,0:T(8,128)S(1)}, f32[2,16,8,128]{3,2,1,0:T(8,128)S(1)}, u32[]{:S(2)}, u32[]{:S(2)}) collective-permute-start(f32[2,16,8,128]{3,2,1,0:T(8,128)S(1)} %edge_rows_away.1), channel_id=1, source_target_pairs={{1,2},{3,4},{5,6},{7,8},{9,10},{11,12},{13,14},{2,1},{4,3},{6,5},{... | collective-permute-start | bytes 393224 | tf_op jit(solution)/shard_map/ppermute | solution.py:465
  48.9 2.6 %copy-start.3 = (bf16[768,256]{1,0:T(8,128)(2,1)S(1)}, bf16[768,256]{1,0:T(8,128)(2,1)}, u32[]{:S(2)}) copy-start(bf16[768,256]{1,0:T(8,128)(2,1)} %constant.30.clone.refs_9_) | copy-start | bytes 1179652
  48.9 2.6 %copy-start.4 = (bf16[512,256]{1,0:T(8,128)(2,1)S(1)}, bf16[512,256]{1,0:T(8,128)(2,1)}, u32[]{:S(2)}) copy-start(bf16[512,256]{1,0:T(8,128)(2,1)} %constant.34.clone.refs_13_) | copy-start | bytes 786436
  48.9 2.6 %copy-start.5 = (bf16[64,192]{1,0:T(8,128)(2,1)S(1)}, bf16[64,192]{1,0:T(8,128)(2,1)}, u32[]{:S(2)}) copy-start(bf16[64,192]{1,0:T(8,128)(2,1)} %constant.32.clone.refs_11_) | copy-start | bytes 73732
  48.9 2.6 %copy-start.6 = (bf16[64,192]{1,0:T(8,128)(2,1)S(1)}, bf16[64,192]{1,0:T(8,128)(2,1)}, u32[]{:S(2)}) copy-start(bf16[64,192]{1,0:T(8,128)(2,1)} %constant.31.clone.refs_10_) | copy-start | bytes 73732
  49.0 2.5 %collective-permute-start = (f32[2,16,8,128]{3,2,1,0:T(8,128)S(1)}, f32[2,16,8,128]{3,2,1,0:T(8,128)S(1)}, u32[]{:S(2)}, u32[]{:S(2)}) collective-permute-start(f32[2,16,8,128]{3,2,1,0:T(8,128)S(1)} %edge_rows_near.1), channel_id=1, source_target_pairs={{0,1},{1,0},{2,3},{3,2},{4,5},{5,4},{6,7},{7,6},{8,9},{9,8},{10,11... | collective-permute-start | bytes 393224 | tf_op jit(solution)/shard_map/ppermute | solution.py:467

commit v4 on v3

--- a/solution.py
+++ b/solution.py
@@ -15,10 +15,10 @@
 LANES = 128
 BLOCK = 256
 OWN_GROUP = 16
-LATE_GROUPS = 4
+LATE_GROUPS = 3
 EARLY_GROUPS = 4
 EDGE_GROUP = 8
-OUT_TILES = 4
+OUT_TILES = 2
 VMEM = pl.BlockSpec(memory_space=pltpu.VMEM)
 SMEM = pl.BlockSpec(memory_space=pltpu.SMEM)
 PARAMS = pltpu.CompilerParams(vmem_limit_bytes=40 * 1024 * 1024)
@@ -101,26 +101,33 @@
 
         @pl.when(core_ref[0] == 0)
         def _():
-            n = count // LATE_GROUPS
-            for g in range(LATE_GROUPS):
-                start(g * n, g * n + n, in_sem.at[g])
+            ends = [count * (g + 1) // LATE_GROUPS for g in range(LATE_GROUPS)]
+            for g, (first, last) in enumerate(zip([0] + ends, ends)):
+                start(first, last, in_sem.at[g])
                 if g == 0:
                     fill()
-                wait(g * n, g * n + n, in_sem.at[g])
-                copy = out(g * n, g * n + n, out_sem.at[g])
+                wait(first, last, in_sem.at[g])
+                copy = out(first, last, out_sem.at[g])
                 copy.start()
                 copy.wait()
 
         @pl.when(core_ref[0] != 0)
         def _():
             n = count // EARLY_GROUPS
+            copies = []
+
+            def send(groups, rows, sem):
+                copy = pltpu.make_async_copy(held_ref.at[groups, rows], o_ref.at[groups, rows], sem)
+                copy.start()
+                copies.append(copy)
+
             for g in range(EARLY_GROUPS):
                 start(g * n, g * n + n, in_sem.at[g])
-            fill()
-            copies = [out(g * n, g * n + n, out_sem.at[g]) for g in range(EARLY_GROUPS)]
             for g in range(EARLY_GROUPS):
                 wait(g * n, g * n + n, in_sem.at[g])
-                copies[g].start()
+                send(slice(g * n, g * n + n), slice(0, 128), out_sem.at[g])
+            fill()
+            send(slice(0, count), slice(128, 136), out_sem.at[EARLY_GROUPS])
             for copy in copies:
                 copy.wait()
 
@@ -135,7 +142,7 @@
             pltpu.VMEM((count, 136, LANES), F32),
             pltpu.SemaphoreType.DMA,
             pltpu.SemaphoreType.DMA((max(LATE_GROUPS, EARLY_GROUPS),)),
-            pltpu.SemaphoreType.DMA((max(LATE_GROUPS, EARLY_GROUPS),)),
+            pltpu.SemaphoreType.DMA((max(LATE_GROUPS, EARLY_GROUPS + 1),)),
         ],
         compiler_params=pltpu.CompilerParams(vmem_limit_bytes=60 * 1024 * 1024),
         cost_estimate=cost(0, 2 << 20),

time: 55.1 us -> 55 us (level)
  blocking collectives: 34.4 us -> 36 us
  starting transfers between devices: 9.55 us -> 7.96 us
    ppermute x1, starting transfers between devices: 9.12 us -> 7.53 us  [on_device(): away = lax.ppermute(edge_rows(slc, second, core, mark, False), 'rows', far)]
    all_to_all x1, blocking collectives: 19.3 us -> 20.7 us  [on_device(): held = lax.all_to_all(spread_chunks(slc, pair_index, core), 'acq', 0, 0)]
where the time goes in v4:
time: 55 us; the launch traced here: 54.6 us
  blocking collectives  36 us (65%)
  Pallas kernels  8.47 us (15%)
  starting transfers between devices  7.96 us (14%)
  waiting for transfers between devices  2.05 us (4%)
    all_to_all x1, blocking collectives, on_device(): held = lax.all_to_all(spread_chunks(slc, pair_index, core), 'acq', 0, 0)  20.7 us
    all_to_all x1, blocking collectives, on_device(): second = lax.all_to_all(pick_chunks(held), 'acq', 0, 0)  15.2 us
    ppermute x1, starting transfers between devices, on_device(): away = lax.ppermute(edge_rows(slc, second, core, mark, False), 'rows', far)  7.53 us
    pallas_call x1, Pallas kernels, with_edges(): pl.pallas_call(kernel, out_shape=jax.ShapeDtypeStruct((1, 3, 32, BLOCK *...  3.1 us
    pallas_call x2, Pallas kernels, own_part(): pl.pallas_call(kernel, out_shape=(jax.ShapeDtypeStruct((2 * count, 32, BL...  3.09 us
    ppermute x1, waiting for transfers between devices, on_device(): away = lax.ppermute(edge_rows(slc, second, core, mark, False), 'rows', far)  2.05 us
    pallas_call x1, Pallas kernels, spread_chunks(): pl.pallas_call(kernel, out_shape=jax.ShapeDtypeStruct((count, 136, LANES)...  2 us
  transfers between devices with their start and end apart: 2, of which 1 were waited for; matrix products, arithmetic and copies ran while one was open for 0% of the time, Pallas kernels for 0%

profile of v4, /device:TPU:97, one launch (start us, length us, event | category | flops | bytes accessed | tf_op | source)
XLA Modules:
  0.0 54.6 jit_solution(14672314909788524079)
XLA Ops:
  0.0 2.0 %spread_chunks.1 = f32[16,136,128]{2,1,0:T(8,128)} custom-call(s32[1]{0:T(128)} %bitcast.core_ref, f32[1,2,32,4096]{3,2,1,0:T(8,128)} %a_ref.7, s32[1,2]{1,0:T(1,128)} %pair_ref.1), custom_call_target="tpu_custom_call" | custom-call | bytes 2097152 | tf_op jit(solution)/shard_map/spread_chunks/pallas_call | solution.py:135
  2.0 20.7 %all_to_all.10.v_ref = f32[16,136,128]{2,1,0:T(8,128)S(1)} all-to-all(f32[16,136,128]{2,1,0:T(8,128)} %spread_chunks.1), channel_id=1, replica_groups=mesh['acq'=16,'rows'=16] {'acq'}, dimensions={0} | all-to-all | bytes 2228224 | tf_op jit(solution)/shard_map/all_to_all | solution.py:469
  22.7 0.1 pick_chunks.1
  22.8 0.0 copy-start
  22.8 0.0 copy-start.1
  22.9 0.0 copy-start.2
  22.9 15.2 %all_to_all.11.b_ref = f32[16,128,128]{2,1,0:T(8,128)S(1)} all-to-all(f32[16,128,128]{2,1,0:T(8,128)S(1)} %pick_chunks.1), channel_id=1, replica_groups=mesh['acq'=16,'rows'=16] {'acq'}, dimensions={0} | all-to-all | bytes 2097152 | tf_op jit(solution)/shard_map/all_to_all | solution.py:470
  38.1 0.0 copy-done
  38.1 0.0 copy-done.1
  38.1 0.0 copy-done.2
  38.1 3.1 %own_part.3 = (f32[32,32,256]{2,1,0:T(8,128)S(1)}, f32[16,32,256]{2,1,0:T(8,128)S(1)}, f32[32,4096]{1,0:T(8,128)S(1)}, f32[8,128]{1,0:T(8,128)S(1)}) custom-call(s32[1]{0:T(128)} %bitcast.core_ref, f32[1,2,32,4096]{3,2,1,0:T(8,128)S(1)} %copy-done, f32[16,128,128]{2,1,0:T(8,128)S(1)} %all_to_all.11.b_ref, bf16[1024,256]{1,0:T(8,128)(2,1)S(1)} %copy-done.1, ...), custom_call_target="tpu_custom_call" | custom-call | flops 4294967296 | bytes 12582912 | tf_op jit(solution)/shard_map/own_part/pallas_call | solution.py:299
  41.2 0.1 edge_rows_away.1
  41.3 7.5 %collective-permute-start.1 = (f32[2,16,8,128]{3,2,1,0:T(8,128)S(1)}, f32[2,16,8,128]{3,2,1,0:T(8,128)S(1)}, u32[]{:S(2)}, u32[]{:S(2)}) collective-permute-start(f32[2,16,8,128]{3,2,1,0:T(8,128)S(1)} %edge_rows_away.1), channel_id=1, source_target_pairs={{1,2},{3,4},{5,6},{7,8},{9,10},{11,12},{13,14},{2,1},{4,3},{6,5},{... | collective-permute-start | bytes 393224 | tf_op jit(solution)/shard_map/ppermute | solution.py:472
  48.9 0.0 copy-start.3
  48.9 0.0 copy-start.4
  48.9 0.0 copy-start.5
  48.9 0.0 copy-start.6
  48.9 0.1 edge_rows_near.1
  49.0 0.4 collective-permute-start
  49.4 2.0 %collective-permute-done.1.refs_7_ = f32[2,16,8,128]{3,2,1,0:T(8,128)S(1)} collective-permute-done((f32[2,16,8,128]{3,2,1,0:T(8,128)S(1)}, f32[2,16,8,128]{3,2,1,0:T(8,128)S(1)}, u32[]{:S(2)}, u32[]{:S(2)}) %collective-permute-start.1) | collective-permute-done | bytes 131104 | tf_op jit(solution)/shard_map/ppermute | solution.py:472
  51.5 0.0 collective-permute-done.refs_6_
  51.5 0.0 copy-done.3
  51.5 0.0 copy-done.4
  51.5 0.0 copy-done.5
  51.5 0.0 copy-done.6
  51.5 3.1 %with_edges.1 = f32[1,3,32,4096]{3,2,1,0:T(8,128)} custom-call(s32[1]{0:T(128)} %bitcast.core_ref, f32[32,32,256]{2,1,0:T(8,128)S(1)} %get-tuple-element.13.refs_0_, f32[16,32,256]{2,1,0:T(8,128)S(1)} %get-tuple-element.14.refs_1_, f32[32,4096]{1,0:T(8,128)S(1)} %get-tuple-element.15.refs_2_, f32[32,32,256]{2,1,0:T(8,128)S(1)} %get-tuple-element.16.refs_3_, ...), custom_call_target="tpu_custom_call" | custom-call | flops 8589934592 | bytes 8388608 | tf_op jit(solution)/shard_map/with_edges/pallas_call | solution.py:437
  (1 shorter events, 0.0 us)
Async XLA Ops:
  22.8 15.3 %copy-start = (f32[1,2,32,4096]{3,2,1,0:T(8,128)S(1)}, f32[1,2,32,4096]{3,2,1,0:T(8,128)}, u32[]{:S(2)}) copy-start(f32[1,2,32,4096]{3,2,1,0:T(8,128)} %a_ref.7) | copy-start | bytes 3145732
  22.8 15.3 %copy-start.1 = (bf16[1024,256]{1,0:T(8,128)(2,1)S(1)}, bf16[1024,256]{1,0:T(8,128)(2,1)}, u32[]{:S(2)}) copy-start(bf16[1024,256]{1,0:T(8,128)(2,1)} %constant.33.clone.w_ref.refs_12_) | copy-start | bytes 1572868
  22.9 15.3 %copy-start.2 = (bf16[768,256]{1,0:T(8,128)(2,1)S(1)}, bf16[768,256]{1,0:T(8,128)(2,1)}, u32[]{:S(2)}) copy-start(bf16[768,256]{1,0:T(8,128)(2,1)} %constant.29.clone.r_ref.refs_8_) | copy-start | bytes 1179652
  41.3 10.2 %collective-permute-start.1 = (f32[2,16,8,128]{3,2,1,0:T(8,128)S(1)}, f32[2,16,8,128]{3,2,1,0:T(8,128)S(1)}, u32[]{:S(2)}, u32[]{:S(2)}) collective-permute-start(f32[2,16,8,128]{3,2,1,0:T(8,128)S(1)} %edge_rows_away.1), channel_id=1, source_target_pairs={{1,2},{3,4},{5,6},{7,8},{9,10},{11,12},{13,14},{2,1},{4,3},{6,5},{... | collective-permute-start | bytes 393224 | tf_op jit(solution)/shard_map/ppermute | solution.py:472
  48.9 2.6 %copy-start.3 = (bf16[768,256]{1,0:T(8,128)(2,1)S(1)}, bf16[768,256]{1,0:T(8,128)(2,1)}, u32[]{:S(2)}) copy-start(bf16[768,256]{1,0:T(8,128)(2,1)} %constant.30.clone.refs_9_) | copy-start | bytes 1179652
  48.9 2.6 %copy-start.4 = (bf16[512,256]{1,0:T(8,128)(2,1)S(1)}, bf16[512,256]{1,0:T(8,128)(2,1)}, u32[]{:S(2)}) copy-start(bf16[512,256]{1,0:T(8,128)(2,1)} %constant.34.clone.refs_13_) | copy-start | bytes 786436
  48.9 2.6 %copy-start.5 = (bf16[64,192]{1,0:T(8,128)(2,1)S(1)}, bf16[64,192]{1,0:T(8,128)(2,1)}, u32[]{:S(2)}) copy-start(bf16[64,192]{1,0:T(8,128)(2,1)} %constant.32.clone.refs_11_) | copy-start | bytes 73732
  48.9 2.6 %copy-start.6 = (bf16[64,192]{1,0:T(8,128)(2,1)S(1)}, bf16[64,192]{1,0:T(8,128)(2,1)}, u32[]{:S(2)}) copy-start(bf16[64,192]{1,0:T(8,128)(2,1)} %constant.31.clone.refs_10_) | copy-start | bytes 73732
  49.0 2.5 %collective-permute-start = (f32[2,16,8,128]{3,2,1,0:T(8,128)S(1)}, f32[2,16,8,128]{3,2,1,0:T(8,128)S(1)}, u32[]{:S(2)}, u32[]{:S(2)}) collective-permute-start(f32[2,16,8,128]{3,2,1,0:T(8,128)S(1)} %edge_rows_near.1), channel_id=1, source_target_pairs={{0,1},{1,0},{2,3},{3,2},{4,5},{5,4},{6,7},{7,6},{8,9},{9,8},{10,11... | collective-permute-start | bytes 393224 | tf_op jit(solution)/shard_map/ppermute | solution.py:474

commit v5 on v4

--- a/solution.py
+++ b/solution.py
@@ -219,8 +219,12 @@
 
 def box_columns(high_ref, low_ref, band, start, n):
     rows = n * high_ref.shape[1]
-    parts = [ref[start + d : start + d + n].reshape(rows, BLOCK) for d in range(2) for ref in (high_ref, low_ref)]
-    return jnp.dot(jnp.concatenate(parts, axis=1), band, preferred_element_type=F32)
+
+    def part(ref, d):
+        lanes = band[2 * BLOCK * d : 2 * BLOCK * d + BLOCK]
+        return jnp.dot(ref[start + d : start + d + n].reshape(rows, BLOCK), lanes, preferred_element_type=F32)
+
+    return (part(high_ref, 0) + part(low_ref, 0)) + (part(high_ref, 1) + part(low_ref, 1))
 
 
 def staggered(count, group, stages):

time: 55 us -> 55.1 us (level)
  no operation moved by 1% of the time
where the time goes in v5:
time: 55.1 us; the launch traced here: 54.7 us
  blocking collectives  36 us (65%)
  Pallas kernels  8.45 us (15%)
  starting transfers between devices  7.96 us (14%)
  waiting for transfers between devices  2.11 us (4%)
    all_to_all x1, blocking collectives, on_device(): held = lax.all_to_all(spread_chunks(slc, pair_index, core), 'acq', 0, 0)  20.7 us
    all_to_all x1, blocking collectives, on_device(): second = lax.all_to_all(pick_chunks(held), 'acq', 0, 0)  15.2 us
    ppermute x1, starting transfers between devices, on_device(): away = lax.ppermute(edge_rows(slc, second, core, mark, False), 'rows', far)  7.59 us
    pallas_call x1, Pallas kernels, with_edges(): pl.pallas_call(kernel, out_shape=jax.ShapeDtypeStruct((1, 3, 32, BLOCK *...  3.15 us
    pallas_call x2, Pallas kernels, own_part(): pl.pallas_call(kernel, out_shape=(jax.ShapeDtypeStruct((2 * count, 32, BL...  3.03 us
    ppermute x1, waiting for transfers between devices, on_device(): away = lax.ppermute(edge_rows(slc, second, core, mark, False), 'rows', far)  2.11 us
    pallas_call x1, Pallas kernels, spread_chunks(): pl.pallas_call(kernel, out_shape=jax.ShapeDtypeStruct((count, 136, LANES)...  2 us
  transfers between devices with their start and end apart: 2, of which 1 were waited for; matrix products, arithmetic and copies ran while one was open for 0% of the time, Pallas kernels for 0%

profile of v5, /device:TPU:97, one launch (start us, length us, event | category | flops | bytes accessed | tf_op | source)
XLA Modules:
  0.0 54.7 jit_solution(17840689588680916781)
XLA Ops:
  0.0 2.0 %spread_chunks.1 = f32[16,136,128]{2,1,0:T(8,128)} custom-call(s32[1]{0:T(128)} %bitcast.core_ref, f32[1,2,32,4096]{3,2,1,0:T(8,128)} %a_ref.7, s32[1,2]{1,0:T(1,128)} %pair_ref.1), custom_call_target="tpu_custom_call" | custom-call | bytes 2097152 | tf_op jit(solution)/shard_map/spread_chunks/pallas_call | solution.py:135
  2.0 20.7 %all_to_all.10.v_ref = f32[16,136,128]{2,1,0:T(8,128)S(1)} all-to-all(f32[16,136,128]{2,1,0:T(8,128)} %spread_chunks.1), channel_id=1, replica_groups=mesh['acq'=16,'rows'=16] {'acq'}, dimensions={0} | all-to-all | bytes 2228224 | tf_op jit(solution)/shard_map/all_to_all | solution.py:473
  22.7 0.1 pick_chunks.1
  22.8 0.0 copy-start
  22.8 0.0 copy-start.1
  22.9 0.0 copy-start.2
  22.9 15.2 %all_to_all.11.b_ref = f32[16,128,128]{2,1,0:T(8,128)S(1)} all-to-all(f32[16,128,128]{2,1,0:T(8,128)S(1)} %pick_chunks.1), channel_id=1, replica_groups=mesh['acq'=16,'rows'=16] {'acq'}, dimensions={0} | all-to-all | bytes 2097152 | tf_op jit(solution)/shard_map/all_to_all | solution.py:474
  38.1 0.0 copy-done
  38.1 0.0 copy-done.1
  38.1 0.0 copy-done.2
  38.1 3.0 %own_part.3 = (f32[32,32,256]{2,1,0:T(8,128)S(1)}, f32[16,32,256]{2,1,0:T(8,128)S(1)}, f32[32,4096]{1,0:T(8,128)S(1)}, f32[8,128]{1,0:T(8,128)S(1)}) custom-call(s32[1]{0:T(128)} %bitcast.core_ref, f32[1,2,32,4096]{3,2,1,0:T(8,128)S(1)} %copy-done, f32[16,128,128]{2,1,0:T(8,128)S(1)} %all_to_all.11.b_ref, bf16[1024,256]{1,0:T(8,128)(2,1)S(1)} %copy-done.1, ...), custom_call_target="tpu_custom_call" | custom-call | flops 4294967296 | bytes 12582912 | tf_op jit(solution)/shard_map/own_part/pallas_call | solution.py:303
  41.1 0.1 edge_rows_away.1
  41.2 7.6 %collective-permute-start.1 = (f32[2,16,8,128]{3,2,1,0:T(8,128)S(1)}, f32[2,16,8,128]{3,2,1,0:T(8,128)S(1)}, u32[]{:S(2)}, u32[]{:S(2)}) collective-permute-start(f32[2,16,8,128]{3,2,1,0:T(8,128)S(1)} %edge_rows_away.1), channel_id=1, source_target_pairs={{1,2},{3,4},{5,6},{7,8},{9,10},{11,12},{13,14},{2,1},{4,3},{6,5},{... | collective-permute-start | bytes 393224 | tf_op jit(solution)/shard_map/ppermute | solution.py:476
  48.9 0.0 copy-start.3
  48.9 0.0 copy-start.4
  48.9 0.0 copy-start.5
  48.9 0.0 copy-start.6
  48.9 0.1 edge_rows_near.1
  49.0 0.4 collective-permute-start
  49.4 2.1 %collective-permute-done.1.refs_7_ = f32[2,16,8,128]{3,2,1,0:T(8,128)S(1)} collective-permute-done((f32[2,16,8,128]{3,2,1,0:T(8,128)S(1)}, f32[2,16,8,128]{3,2,1,0:T(8,128)S(1)}, u32[]{:S(2)}, u32[]{:S(2)}) %collective-permute-start.1) | collective-permute-done | bytes 131104 | tf_op jit(solution)/shard_map/ppermute | solution.py:476
  51.5 0.0 collective-permute-done.refs_6_
  51.5 0.0 copy-done.3
  51.5 0.0 copy-done.4
  51.5 0.0 copy-done.5
  51.5 0.0 copy-done.6
  51.5 3.2 %with_edges.1 = f32[1,3,32,4096]{3,2,1,0:T(8,128)} custom-call(s32[1]{0:T(128)} %bitcast.core_ref, f32[32,32,256]{2,1,0:T(8,128)S(1)} %get-tuple-element.13.refs_0_, f32[16,32,256]{2,1,0:T(8,128)S(1)} %get-tuple-element.14.refs_1_, f32[32,4096]{1,0:T(8,128)S(1)} %get-tuple-element.15.refs_2_, f32[32,32,256]{2,1,0:T(8,128)S(1)} %get-tuple-element.16.refs_3_, ...), custom_call_target="tpu_custom_call" | custom-call | flops 8589934592 | bytes 8388608 | tf_op jit(solution)/shard_map/with_edges/pallas_call | solution.py:441
  (1 shorter events, 0.0 us)
Async XLA Ops:
  22.8 15.3 %copy-start = (f32[1,2,32,4096]{3,2,1,0:T(8,128)S(1)}, f32[1,2,32,4096]{3,2,1,0:T(8,128)}, u32[]{:S(2)}) copy-start(f32[1,2,32,4096]{3,2,1,0:T(8,128)} %a_ref.7) | copy-start | bytes 3145732
  22.8 15.3 %copy-start.1 = (bf16[1024,256]{1,0:T(8,128)(2,1)S(1)}, bf16[1024,256]{1,0:T(8,128)(2,1)}, u32[]{:S(2)}) copy-start(bf16[1024,256]{1,0:T(8,128)(2,1)} %constant.33.clone.w_ref.refs_12_) | copy-start | bytes 1572868
  22.9 15.3 %copy-start.2 = (bf16[768,256]{1,0:T(8,128)(2,1)S(1)}, bf16[768,256]{1,0:T(8,128)(2,1)}, u32[]{:S(2)}) copy-start(bf16[768,256]{1,0:T(8,128)(2,1)} %constant.29.clone.r_ref.refs_8_) | copy-start | bytes 1179652
  41.2 10.2 %collective-permute-start.1 = (f32[2,16,8,128]{3,2,1,0:T(8,128)S(1)}, f32[2,16,8,128]{3,2,1,0:T(8,128)S(1)}, u32[]{:S(2)}, u32[]{:S(2)}) collective-permute-start(f32[2,16,8,128]{3,2,1,0:T(8,128)S(1)} %edge_rows_away.1), channel_id=1, source_target_pairs={{1,2},{3,4},{5,6},{7,8},{9,10},{11,12},{13,14},{2,1},{4,3},{6,5},{... | collective-permute-start | bytes 393224 | tf_op jit(solution)/shard_map/ppermute | solution.py:476
  48.9 2.6 %copy-start.3 = (bf16[768,256]{1,0:T(8,128)(2,1)S(1)}, bf16[768,256]{1,0:T(8,128)(2,1)}, u32[]{:S(2)}) copy-start(bf16[768,256]{1,0:T(8,128)(2,1)} %constant.30.clone.refs_9_) | copy-start | bytes 1179652
  48.9 2.6 %copy-start.4 = (bf16[512,256]{1,0:T(8,128)(2,1)S(1)}, bf16[512,256]{1,0:T(8,128)(2,1)}, u32[]{:S(2)}) copy-start(bf16[512,256]{1,0:T(8,128)(2,1)} %constant.34.clone.refs_13_) | copy-start | bytes 786436
  48.9 2.6 %copy-start.5 = (bf16[64,192]{1,0:T(8,128)(2,1)S(1)}, bf16[64,192]{1,0:T(8,128)(2,1)}, u32[]{:S(2)}) copy-start(bf16[64,192]{1,0:T(8,128)(2,1)} %constant.32.clone.refs_11_) | copy-start | bytes 73732
  48.9 2.6 %copy-start.6 = (bf16[64,192]{1,0:T(8,128)(2,1)S(1)}, bf16[64,192]{1,0:T(8,128)(2,1)}, u32[]{:S(2)}) copy-start(bf16[64,192]{1,0:T(8,128)(2,1)} %constant.31.clone.refs_10_) | copy-start | bytes 73732
  49.0 2.5 %collective-permute-start = (f32[2,16,8,128]{3,2,1,0:T(8,128)S(1)}, f32[2,16,8,128]{3,2,1,0:T(8,128)S(1)}, u32[]{:S(2)}, u32[]{:S(2)}) collective-permute-start(f32[2,16,8,128]{3,2,1,0:T(8,128)S(1)} %edge_rows_near.1), channel_id=1, source_target_pairs={{0,1},{1,0},{2,3},{3,2},{4,5},{5,4},{6,7},{7,6},{8,9},{9,8},{10,11... | collective-permute-start | bytes 393224 | tf_op jit(solution)/shard_map/ppermute | solution.py:478

commit v6 on v4

--- a/solution.py
+++ b/solution.py
@@ -17,7 +17,7 @@
 OWN_GROUP = 16
 LATE_GROUPS = 3
 EARLY_GROUPS = 4
-EDGE_GROUP = 8
+EDGE_GROUPS = {0: 10, 10: 6}
 OUT_TILES = 2
 VMEM = pl.BlockSpec(memory_space=pltpu.VMEM)
 SMEM = pl.BlockSpec(memory_space=pltpu.SMEM)
@@ -223,8 +223,7 @@
     return jnp.dot(jnp.concatenate(parts, axis=1), band, preferred_element_type=F32)
 
 
-def staggered(count, group, stages):
-    starts = list(range(0, count, group))
+def staggered(starts, stages):
     for t in range(len(starts) + len(stages) - 1):
         for s in reversed(range(len(stages))):
             if 0 <= t - s < len(starts):
@@ -294,7 +293,7 @@
             y = jnp.dot(jnp.concatenate([h, l, h], axis=1), r_ref[...], preferred_element_type=F32)
             y_ref[m : m + n] = y.reshape(n, 32, BLOCK)
 
-        staggered(count, group, (row_sums, gamma, transform))
+        staggered(list(range(0, count, group)), (row_sums, gamma, transform))
 
     return pl.pallas_call(
         kernel,
@@ -321,7 +320,6 @@
 
 def with_edges(late, early, halos, core, right, right_inv, left, left_inv, band, mean):
     count = late[1].shape[0]
-    group = EDGE_GROUP
 
     def kernel(core_ref, *refs):
         @pl.when(core_ref[0] == 0)
@@ -367,6 +365,7 @@
             high_ref[j], low_ref[j] = split(part_ref[j])
 
         def gamma(g):
+            group = EDGE_GROUPS[g]
             more = box_columns(high_ref, low_ref, w_ref[...], g, group)
             for j in range(g, g + group):
                 at = 32 * (j - g)
@@ -378,6 +377,9 @@
                 put_tiles(g_ref, j, jnp.where(outer, gr, 0.0), jnp.where(outer, gi, 0.0))
 
         def transform(g):
+            group = EDGE_GROUPS[g]
+            if g + group == count:
+                strips()
             m, n = 2 * g, 2 * group
             h, l = split(g_ref[m : m + n].reshape(8 * n, BLOCK))
             y = jnp.dot(jnp.concatenate([h, l, h], axis=1), r_ref[...], preferred_element_type=F32)
@@ -387,7 +389,14 @@
                 y_ref[m + t, 8:24] = yin_ref[m + t, 8:24]
                 y_ref[m + t, 24:32] = yin_ref[m + t, 24:32] + jnp.where(sub < 4, 0.0, more)
 
+        def strips():
+            for i in range(2):
+                copy = pltpu.make_async_copy(strip_ref.at[i], o_ref.at[0, 0, 24 * i : 24 * i + 8], sem.at[1 + i])
+                copy.start()
+                copies.append(copy)
+
         def forward(g):
+            group = EDGE_GROUPS[g]
             for j in range(g, g + group):
                 h, l = split(get_tiles(y_ref, j))
                 z_ref[j] = jnp.dot(l_ref[...], jnp.concatenate([h, l, h], axis=0), preferred_element_type=F32)
@@ -395,6 +404,7 @@
         sums = {}
 
         def backward(g):
+            group = EDGE_GROUPS[g]
             parts = []
             for j in range(g, g + group):
                 zr, zi = z_ref[j, 0:32], z_ref[j, 32:64]
@@ -410,6 +420,7 @@
             sums[g] = 1.0 / jnp.sum(total.reshape(group, 8, BLOCK), axis=1, keepdims=True)
 
         def finish(g):
+            group = EDGE_GROUPS[g]
             m, n = 2 * g, 2 * group
             h, l = (ref[m : m + n].reshape(32 * n, BLOCK) for ref in (vh_ref, vl_ref))
             out = jnp.dot(jnp.concatenate([h, l, h], axis=1), ri_ref[...], preferred_element_type=F32)
@@ -424,13 +435,8 @@
                     copy = pltpu.make_async_copy(out_ref.at[:, :, cols], o_ref.at[0, 1:3, :, cols], at)
                     copy.start()
                     copies.append(copy)
-            if g + group == count:
-                for i in range(2):
-                    copy = pltpu.make_async_copy(strip_ref.at[i], o_ref.at[0, 0, 24 * i : 24 * i + 8], sem.at[1 + i])
-                    copy.start()
-                    copies.append(copy)
-
-        staggered(count, group, (gamma, transform, forward, backward, finish))
+
+        staggered(list(EDGE_GROUPS), (gamma, transform, forward, backward, finish))
         for copy in copies:
             copy.wait()
 

time: 55 us -> 55 us (level)
  no operation moved by 1% of the time
where the time goes in v6:
time: 55 us; the launch traced here: 54.5 us
  blocking collectives  36 us (65%)
  Pallas kernels  8.39 us (15%)
  starting transfers between devices  7.96 us (14%)
  waiting for transfers between devices  2.05 us (4%)
    all_to_all x1, blocking collectives, on_device(): held = lax.all_to_all(spread_chunks(slc, pair_index, core), 'acq', 0, 0)  20.7 us
    all_to_all x1, blocking collectives, on_device(): second = lax.all_to_all(pick_chunks(held), 'acq', 0, 0)  15.2 us
    ppermute x1, starting transfers between devices, on_device(): away = lax.ppermute(edge_rows(slc, second, core, mark, False), 'rows', far)  7.53 us
    pallas_call x2, Pallas kernels, own_part(): pl.pallas_call(kernel, out_shape=(jax.ShapeDtypeStruct((2 * count, 32, BL...  3.09 us
    pallas_call x1, Pallas kernels, with_edges(): pl.pallas_call(kernel, out_shape=jax.ShapeDtypeStruct((1, 3, 32, BLOCK *...  3.03 us
    ppermute x1, waiting for transfers between devices, on_device(): away = lax.ppermute(edge_rows(slc, second, core, mark, False), 'rows', far)  2.05 us
    pallas_call x1, Pallas kernels, spread_chunks(): pl.pallas_call(kernel, out_shape=jax.ShapeDtypeStruct((count, 136, LANES)...  2 us
  transfers between devices with their start and end apart: 2, of which 1 were waited for; matrix products, arithmetic and copies ran while one was open for 0% of the time, Pallas kernels for 0%

profile of v6, /device:TPU:97, one launch (start us, length us, event | category | flops | bytes accessed | tf_op | source)
XLA Modules:
  0.0 54.5 jit_solution(17811104847880675950)
XLA Ops:
  0.0 2.0 %spread_chunks.1 = f32[16,136,128]{2,1,0:T(8,128)} custom-call(s32[1]{0:T(128)} %bitcast.core_ref, f32[1,2,32,4096]{3,2,1,0:T(8,128)} %a_ref.7, s32[1,2]{1,0:T(1,128)} %pair_ref.1), custom_call_target="tpu_custom_call" | custom-call | bytes 2097152 | tf_op jit(solution)/shard_map/spread_chunks/pallas_call | solution.py:135
  2.0 20.7 %all_to_all.10.v_ref = f32[16,136,128]{2,1,0:T(8,128)S(1)} all-to-all(f32[16,136,128]{2,1,0:T(8,128)} %spread_chunks.1), channel_id=1, replica_groups=mesh['acq'=16,'rows'=16] {'acq'}, dimensions={0} | all-to-all | bytes 2228224 | tf_op jit(solution)/shard_map/all_to_all | solution.py:475
  22.7 0.1 pick_chunks.1
  22.8 0.0 copy-start
  22.8 0.0 copy-start.1
  22.9 0.0 copy-start.2
  22.9 15.2 %all_to_all.11.b_ref = f32[16,128,128]{2,1,0:T(8,128)S(1)} all-to-all(f32[16,128,128]{2,1,0:T(8,128)S(1)} %pick_chunks.1), channel_id=1, replica_groups=mesh['acq'=16,'rows'=16] {'acq'}, dimensions={0} | all-to-all | bytes 2097152 | tf_op jit(solution)/shard_map/all_to_all | solution.py:476
  38.1 0.0 copy-done
  38.1 0.0 copy-done.1
  38.1 0.0 copy-done.2
  38.1 3.1 %own_part.3 = (f32[32,32,256]{2,1,0:T(8,128)S(1)}, f32[16,32,256]{2,1,0:T(8,128)S(1)}, f32[32,4096]{1,0:T(8,128)S(1)}, f32[8,128]{1,0:T(8,128)S(1)}) custom-call(s32[1]{0:T(128)} %bitcast.core_ref, f32[1,2,32,4096]{3,2,1,0:T(8,128)S(1)} %copy-done, f32[16,128,128]{2,1,0:T(8,128)S(1)} %all_to_all.11.b_ref, bf16[1024,256]{1,0:T(8,128)(2,1)S(1)} %copy-done.1, ...), custom_call_target="tpu_custom_call" | custom-call | flops 4294967296 | bytes 12582912 | tf_op jit(solution)/shard_map/own_part/pallas_call | solution.py:298
  41.2 0.1 edge_rows_away.1
  41.3 7.5 %collective-permute-start.1 = (f32[2,16,8,128]{3,2,1,0:T(8,128)S(1)}, f32[2,16,8,128]{3,2,1,0:T(8,128)S(1)}, u32[]{:S(2)}, u32[]{:S(2)}) collective-permute-start(f32[2,16,8,128]{3,2,1,0:T(8,128)S(1)} %edge_rows_away.1), channel_id=1, source_target_pairs={{1,2},{3,4},{5,6},{7,8},{9,10},{11,12},{13,14},{2,1},{4,3},{6,5},{... | collective-permute-start | bytes 393224 | tf_op jit(solution)/shard_map/ppermute | solution.py:478
  48.9 0.0 copy-start.3
  48.9 0.0 copy-start.4
  48.9 0.0 copy-start.5
  48.9 0.0 copy-start.6
  48.9 0.1 edge_rows_near.1
  49.0 0.4 collective-permute-start
  49.4 2.0 %collective-permute-done.1.refs_7_ = f32[2,16,8,128]{3,2,1,0:T(8,128)S(1)} collective-permute-done((f32[2,16,8,128]{3,2,1,0:T(8,128)S(1)}, f32[2,16,8,128]{3,2,1,0:T(8,128)S(1)}, u32[]{:S(2)}, u32[]{:S(2)}) %collective-permute-start.1) | collective-permute-done | bytes 131104 | tf_op jit(solution)/shard_map/ppermute | solution.py:478
  51.5 0.0 collective-permute-done.refs_6_
  51.5 0.0 copy-done.3
  51.5 0.0 copy-done.4
  51.5 0.0 copy-done.5
  51.5 0.0 copy-done.6
  51.5 3.0 %with_edges.1 = f32[1,3,32,4096]{3,2,1,0:T(8,128)} custom-call(s32[1]{0:T(128)} %bitcast.core_ref, f32[32,32,256]{2,1,0:T(8,128)S(1)} %get-tuple-element.13.refs_0_, f32[16,32,256]{2,1,0:T(8,128)S(1)} %get-tuple-element.14.refs_1_, f32[32,4096]{1,0:T(8,128)S(1)} %get-tuple-element.15.refs_2_, f32[32,32,256]{2,1,0:T(8,128)S(1)} %get-tuple-element.16.refs_3_, ...), custom_call_target="tpu_custom_call" | custom-call | flops 8589934592 | bytes 8388608 | tf_op jit(solution)/shard_map/with_edges/pallas_call | solution.py:443
  (1 shorter events, 0.0 us)
Async XLA Ops:
  22.8 15.3 %copy-start = (f32[1,2,32,4096]{3,2,1,0:T(8,128)S(1)}, f32[1,2,32,4096]{3,2,1,0:T(8,128)}, u32[]{:S(2)}) copy-start(f32[1,2,32,4096]{3,2,1,0:T(8,128)} %a_ref.7) | copy-start | bytes 3145732
  22.8 15.3 %copy-start.1 = (bf16[1024,256]{1,0:T(8,128)(2,1)S(1)}, bf16[1024,256]{1,0:T(8,128)(2,1)}, u32[]{:S(2)}) copy-start(bf16[1024,256]{1,0:T(8,128)(2,1)} %constant.33.clone.w_ref.refs_12_) | copy-start | bytes 1572868
  22.9 15.3 %copy-start.2 = (bf16[768,256]{1,0:T(8,128)(2,1)S(1)}, bf16[768,256]{1,0:T(8,128)(2,1)}, u32[]{:S(2)}) copy-start(bf16[768,256]{1,0:T(8,128)(2,1)} %constant.29.clone.r_ref.refs_8_) | copy-start | bytes 1179652
  41.3 10.2 %collective-permute-start.1 = (f32[2,16,8,128]{3,2,1,0:T(8,128)S(1)}, f32[2,16,8,128]{3,2,1,0:T(8,128)S(1)}, u32[]{:S(2)}, u32[]{:S(2)}) collective-permute-start(f32[2,16,8,128]{3,2,1,0:T(8,128)S(1)} %edge_rows_away.1), channel_id=1, source_target_pairs={{1,2},{3,4},{5,6},{7,8},{9,10},{11,12},{13,14},{2,1},{4,3},{6,5},{... | collective-permute-start | bytes 393224 | tf_op jit(solution)/shard_map/ppermute | solution.py:478
  48.9 2.6 %copy-start.3 = (bf16[768,256]{1,0:T(8,128)(2,1)S(1)}, bf16[768,256]{1,0:T(8,128)(2,1)}, u32[]{:S(2)}) copy-start(bf16[768,256]{1,0:T(8,128)(2,1)} %constant.30.clone.refs_9_) | copy-start | bytes 1179652
  48.9 2.6 %copy-start.4 = (bf16[512,256]{1,0:T(8,128)(2,1)S(1)}, bf16[512,256]{1,0:T(8,128)(2,1)}, u32[]{:S(2)}) copy-start(bf16[512,256]{1,0:T(8,128)(2,1)} %constant.34.clone.refs_13_) | copy-start | bytes 786436
  48.9 2.6 %copy-start.5 = (bf16[64,192]{1,0:T(8,128)(2,1)S(1)}, bf16[64,192]{1,0:T(8,128)(2,1)}, u32[]{:S(2)}) copy-start(bf16[64,192]{1,0:T(8,128)(2,1)} %constant.32.clone.refs_11_) | copy-start | bytes 73732
  48.9 2.6 %copy-start.6 = (bf16[64,192]{1,0:T(8,128)(2,1)S(1)}, bf16[64,192]{1,0:T(8,128)(2,1)}, u32[]{:S(2)}) copy-start(bf16[64,192]{1,0:T(8,128)(2,1)} %constant.31.clone.refs_10_) | copy-start | bytes 73732
  49.0 2.5 %collective-permute-start = (f32[2,16,8,128]{3,2,1,0:T(8,128)S(1)}, f32[2,16,8,128]{3,2,1,0:T(8,128)S(1)}, u32[]{:S(2)}, u32[]{:S(2)}) collective-permute-start(f32[2,16,8,128]{3,2,1,0:T(8,128)S(1)} %edge_rows_near.1), channel_id=1, source_target_pairs={{0,1},{1,0},{2,3},{3,2},{4,5},{5,4},{6,7},{7,6},{8,9},{9,8},{10,11... | collective-permute-start | bytes 393224 | tf_op jit(solution)/shard_map/ppermute | solution.py:480
